TPU v7x, 32 devices: a whole 2x2x4 slice. The times are simulated.
32 devices in a mesh: row: 8 (over z, y), col: 4 (over x, core).
Axes of the slice: x: 2, y: 2, z: 4, core: 2. Of those that a mesh axis runs over, the one named last changes fastest.
Arguments:
- points: bfloat16 [64, 16384], P(None, ('row', 'col')), may hold values from -6 to 6
- lengths: float32 [64], replicated, may hold values from 0.5 to 2
- noise_var: float32 [16384], P(('row', 'col')), may hold values from 0.1 to 1
- solution: float32 [16, 16384], P(None, ('row', 'col')), may hold values from -6 to 6
- residual: float32 [16, 16384], P(None, ('row', 'col')), may hold values from -100 to 100
- direction: float32 [16, 16384], P(None, ('row', 'col')), may hold values from -100 to 100
Outputs:
- new_solution: float32 [16, 16384], P(None, ('row', 'col'))
- new_residual: float32 [16, 16384], P(None, ('row', 'col'))
- new_direction: float32 [16, 16384], P(None, ('row', 'col'))
All inputs are finite; a program needn't handle non-finite values.
Results may differ from a plain program's by a relative error of at most 0.0043.
Values may be sent and summed in bfloat16 or wider, within the bound.
No kernel may reach another device: no remote copies, remote signals or barrier semaphores. Data moves between devices by JAX's collectives and lax.ppermute only.
A program may use at most 64 MiB of HBM per device.

v0:
```python
import math

import jax
import jax.numpy as jnp
from jax import lax
from jax.sharding import PartitionSpec as P


def column_squares(scaled):
    values = scaled.astype(jnp.float32)
    return jnp.sum(values * values, axis=0)


def kernel_block(left_cols, left_sq, right_cols, right_sq):
    cross_term = lax.dot_general(
        left_cols, right_cols, (((0,), (0,)), ((), ())), preferred_element_type=jnp.float32
    )
    distance = left_sq[:, None] + right_sq[None, :] - 2.0 * cross_term
    return jnp.exp(-0.5 * distance).astype(jnp.bfloat16)


def grid_image(scaled, narrow_direction):
    row_scaled = lax.all_gather(scaled, "col", axis=1, tiled=True)
    row_sq = column_squares(row_scaled)
    row_count = row_scaled.shape[1]
    zero_start = jnp.zeros((narrow_direction.shape[0], row_count), jnp.float32)
    col_scaled = lax.all_gather(scaled, "row", axis=1, tiled=True)
    col_dir = lax.all_gather(narrow_direction, "row", axis=1, tiled=True)
    col_count = col_scaled.shape[1]
    block_width = math.gcd(col_count, row_count)

    def one_block(block_index, accumulated):
        begin = block_index * block_width
        part_scaled = lax.dynamic_slice_in_dim(col_scaled, begin, block_width, 1)
        part_dir = lax.dynamic_slice_in_dim(col_dir, begin, block_width, 1)
        kernel_tile = kernel_block(part_scaled, column_squares(part_scaled), row_scaled, row_sq)
        return accumulated + jnp.dot(part_dir, kernel_tile, preferred_element_type=jnp.float32)

    partial_value = lax.fori_loop(0, col_count // block_width, one_block, zero_start)
    return lax.psum_scatter(partial_value, "col", scatter_dimension=1, tiled=True)


def local(points, lengths, noise_var, solution, residual, direction):
    scaled = (points.astype(jnp.float32) / lengths[:, None]).astype(jnp.bfloat16)
    narrow_direction = direction.astype(jnp.bfloat16)
    kernel_part = grid_image(scaled, narrow_direction)
    image_field = kernel_part + noise_var[None, :] * direction
    norm_old, curvature = lax.psum(
        (jnp.sum(residual * residual, axis=1), jnp.sum(direction * image_field, axis=1)),
        ("row", "col"),
    )
    step_size = norm_old / curvature
    new_residual = residual - step_size[:, None] * image_field
    norm_new = lax.psum(jnp.sum(new_residual * new_residual, axis=1), ("row", "col"))
    new_solution = solution + step_size[:, None] * direction
    new_direction = new_residual + (norm_new / norm_old)[:, None] * direction
    return (new_solution, new_residual, new_direction)


def solution(mesh):
    placed = (
        P(None, ("row", "col")),
        P(),
        P(("row", "col")),
        P(None, ("row", "col")),
        P(None, ("row", "col")),
        P(None, ("row", "col")),
    )
    return jax.shard_map(
        local,
        mesh=mesh,
        in_specs=placed,
        out_specs=(P(None, ("row", "col")), P(None, ("row", "col")), P(None, ("row", "col"))),
        check_vma=False,
    )
```

profile of v0, /device:TPU:0, one launch (start us, length us, event | category | flops | bytes accessed | tf_op | source)
XLA Modules:
  0.0 198.5 jit_solution(6511651485207780408)
XLA Ops:
  7.2 0.0 reduce-scatter.2.cloned.1.call-start
  7.2 0.9 divide_convert_fusion
  8.1 0.0 copy-start
  8.2 7.2 %all_gather.11 = bf16[64,2048]{1,0:T(8,128)(2,1)S(1)} all-gather(bf16[64,512]{1,0:T(8,128)(2,1)S(1)} %divide_convert_fusion), channel_id=1, replica_groups=mesh['row'=8,'col'=4] {'col'}, dimensions={1}, use_global_device_ids=true | all-gather | bytes 327680 | tf_op jit(solution)/shard_map/all_gather | solution.py:23
  15.3 31.9 %all_gather.10 = bf16[64,4096]{1,0:T(8,128)(2,1)S(1)} all-gather(bf16[64,512]{1,0:T(8,128)(2,1)S(1)} %divide_convert_fusion), channel_id=1, replica_groups=mesh['row'=8,'col'=4] {'row'}, dimensions={1}, use_global_device_ids=true | all-gather | bytes 589824 | tf_op jit(solution)/shard_map/all_gather | solution.py:27
  47.3 0.1 multiply_reduce_fusion.1
  47.4 0.0 copy-done
  47.4 30.5 %all_gather.9 = bf16[16,4096]{1,0:T(8,128)(2,1)S(1)} all-gather(bf16[16,512]{1,0:T(8,128)(2,1)S(1)} %convert_element_type.26), channel_id=1, replica_groups=mesh['row'=8,'col'=4] {'row'}, dimensions={1}, use_global_device_ids=true | all-gather | bytes 147456 | tf_op jit(solution)/shard_map/all_gather | solution.py:28
  77.9 9.1 %while.14 = (s32[]{:T(128)}, f32[16,2048]{1,0:T(8,128)S(1)}, bf16[16,4096]{1,0:T(8,128)(2,1)S(1)}, bf16[64,4096]{1,0:T(8,128)(2,1)S(1)}, f32[2048]{0:T(1024)S(1)...) while((s32[]{:T(128)}, f32[16,2048]{1,0:T(8,128)S(1)}, ...), condition=%wide.region_5.0_spmd.clone, body=%wide.region_3.5_spmd.clone.sunk | while | flops 692516864 | bytes 1140384 | solution.py:39
  77.9 0.1 multiply_reduce_fusion.6
  78.0 4.5 %fusion.17 = f32[16,2048]{1,0:T(8,128)S(1)} fusion(bf16[64,2048]{1,0:T(8,128)(2,1)S(1)} %get-tuple-element.213, f32[2048]{0:T(1024)S(1)} %get-tuple-element.212, f32[2048]{0:T(1024)S(1)} %multiply_reduce_fusion.6, bf16[64,4096]{1,0:T(8,128)(2,1)S(1)} %get-tuple-element.211, s32[]{:T(128)S(6)} %select_n.10, f32[16,2048]{1,0:T(8,128)S(1)} %get-tuple-element.199, ...), kind=kOutput, calls=%fused_computation.2.clone.1 | convolution fusion | flops 692125696 | bytes 869888 | tf_op jit(solution)/shard_map/while/body/eval_jaxpr/dot_general | solution.py:37
  82.5 0.1 multiply_reduce_fusion.6
  82.6 4.5 %fusion.17 = f32[16,2048]{1,0:T(8,128)S(1)} fusion(bf16[64,2048]{1,0:T(8,128)(2,1)S(1)} %get-tuple-element.213, f32[2048]{0:T(1024)S(1)} %get-tuple-element.212, f32[2048]{0:T(1024)S(1)} %multiply_reduce_fusion.6, bf16[64,4096]{1,0:T(8,128)(2,1)S(1)} %get-tuple-element.211, s32[]{:T(128)S(6)} %select_n.10, f32[16,2048]{1,0:T(8,128)S(1)} %get-tuple-element.199, ...), kind=kOutput, calls=%fused_computation.2.clone.1 | convolution fusion | flops 692125696 | bytes 869888 | tf_op jit(solution)/shard_map/while/body/eval_jaxpr/dot_general | solution.py:37
  87.0 0.6 copy-done.3
  87.7 0.0 reduce-scatter.2.cloned.1.call-update
  87.7 0.0 copy-done.2
  87.7 0.1 multiply_reduce_fusion.4
  87.8 20.3 %reduce-scatter.2.cloned.1.call-done = f32[16,512]{1,0:T(8,128)} async-done(((f32[16,2048]{1,0:T(8,128)}), f32[16,512]{1,0:T(8,128)}) %reduce-scatter.2.cloned.1.call-update) | async-done | bytes 32784 | tf_op jit(solution)/shard_map/reduce_scatter | solution.py:40
  108.2 0.0 copy-done.5
  108.2 0.9 multiply_reduce_fusion.3
  109.1 39.3 %all-reduce = (f32[16]{0:T(128)S(1)}, f32[16]{0:T(128)S(1)}) all-reduce(f32[16]{0:T(128)S(1)} %multiply_reduce_fusion.4, f32[16]{0:T(128)S(1)} %multiply_reduce_fusion.3), channel_id=1, replica_groups=mesh['row'=8,'col'=4] {'row','col'}, use_global_device_ids=true, to_apply=%region_1.2 | all-reduce | flops 32 | bytes 256 | tf_op jit(solution)/shard_map/psum | solution.py:48
  148.4 1.6 multiply_reduce_fusion.2
  150.0 41.0 %psum.23 = f32[16]{0:T(128)S(1)} all-reduce(f32[16]{0:T(128)S(1)} %get-tuple-element.148), channel_id=1, replica_groups=mesh['row'=8,'col'=4] {'row','col'}, use_global_device_ids=true, to_apply=%region_10.0 | all-reduce | flops 16 | bytes 128 | tf_op jit(solution)/shard_map/psum | solution.py:54
  191.0 0.7 multiply_add_fusion
  (11 shorter events, 0.0 us)
Async XLA Ops:
  7.2 101.0 %reduce-scatter.2.cloned.1.call-start = ((), (), s32[]{:S(2)}) async-start(), calls=%async_computation.1 | async-start | bytes 163840 | tf_op jit(solution)/shard_map/reduce_scatter | solution.py:40
  8.1 39.2 %copy-start = (f32[16,512]{1,0:T(8,128)S(1)}, f32[16,512]{1,0:T(8,128)}, u32[]{:S(2)}) copy-start(f32[16,512]{1,0:T(8,128)} %param.13) | copy-start | bytes 98308
  77.9 9.8 %copy-start.2 = (f32[16,512]{1,0:T(8,128)S(1)}, f32[16,512]{1,0:T(8,128)}, u32[]{:S(2)}) copy-start(f32[16,512]{1,0:T(8,128)} %param.12) | copy-start | bytes 98308
  77.9 30.3 %copy-start.5 = (f32[512]{0:T(512)S(1)}, f32[512]{0:T(512)}, u32[]{:S(2)}) copy-start(f32[512]{0:T(512)} %param.10) | copy-start | bytes 6148
  77.9 70.5 %copy-start.4 = (f32[16,512]{1,0:T(8,128)S(1)}, f32[16,512]{1,0:T(8,128)}, u32[]{:S(2)}) copy-start(f32[16,512]{1,0:T(8,128)} %param.11) | copy-start | bytes 98308
  87.0 0.6 copy-start.3
  150.0 41.7 %copy-start.1 = (f32[16,512]{1,0:T(8,128)}, f32[16,512]{1,0:T(8,128)S(1)}, u32[]{:S(2)}) copy-start(f32[16,512]{1,0:T(8,128)S(1)} %get-tuple-element.149) | copy-start | bytes 98308
Sparse Core Ops, SparseCore 0:
  87.8 20.3 reduce-scatter.1
where the time goes:
time: 199 us
  blocking collectives  150 us (75%)
  waiting for transfers between devices  20.4 us (10%)
  between operations  14.1 us (7%)
  matrix products  8.94 us (4%)
  other arithmetic  4.41 us (2%)
    psum x1, blocking collectives, local(): lax.psum(jnp.sum(new_residual * new_residual, axis=1), ('row', 'col'))  41 us
    psum x1, blocking collectives, local(): lax.psum((jnp.sum(residual * residual, axis=1), jnp.sum(direction * image...  39.3 us
    all_gather x1, blocking collectives, grid_image(): col_scaled = lax.all_gather(scaled, 'row', axis=1, tiled=True)  31.9 us
    all_gather x1, blocking collectives, grid_image(): col_dir = lax.all_gather(narrow_direction, 'row', axis=1, tiled=True)  30.5 us
    reduce_scatter x1, waiting for transfers between devices, grid_image(): lax.psum_scatter(partial_value, 'col', scatter_dimension=1, tiled=True)  20.3 us
    dot_general x2, matrix products, one_block(): jnp.dot(part_dir, kernel_tile, preferred_element_type=jnp.float32)  8.94 us
    all_gather x1, blocking collectives, grid_image(): row_scaled = lax.all_gather(scaled, 'col', axis=1, tiled=True)  7.19 us
  transfers between devices with their start and end apart: 1, of which 1 were waited for; matrix products, arithmetic and copies ran while one was open for 0% of the time, Pallas kernels for 0%

commit v1 on v0

v1 whole, which is shorter than its diff:
```python
import functools

import jax
import jax.numpy as jnp
from jax import lax
from jax.experimental import pallas as pl
from jax.experimental.pallas import tpu as pltpu
from jax.sharding import PartitionSpec as P

AXES = ("row", "col")
X, Y = 2, 4
CORE = 1
LINE = 8
LOG2E = 1.4426950408889634
TAIL = 16
UNROLL = 16
VMEM_LIMIT = 24 * 1024 * 1024


def params():
    return pltpu.CompilerParams(vmem_limit_bytes=VMEM_LIMIT)


def three_pieces(value):
    high = value.astype(jnp.bfloat16).astype(jnp.float32)
    rest = value - high
    middle = rest.astype(jnp.bfloat16).astype(jnp.float32)
    return high, middle, rest - middle


def tail_rows(squares, first):
    count = squares.shape[1]
    high, middle, low = three_pieces(-0.5 * squares)
    at = lax.broadcasted_iota(jnp.int32, (TAIL, count), 0)
    start = 0 if first else 3
    tail = jnp.where(at < 6, 1.0, 0.0)
    tail = jnp.where(at == start, high, tail)
    tail = jnp.where(at == start + 1, middle, tail)
    tail = jnp.where(at == start + 2, low, tail)
    return tail


def scaled_of(points, lengths):
    return (points.astype(jnp.float32) / lengths).astype(jnp.bfloat16)


def squares_of(scaled):
    values = scaled.astype(jnp.float32)
    return jnp.sum(values * values, axis=0, keepdims=True)


def side_of(points, lengths, first):
    scaled = scaled_of(points, lengths)
    tail = tail_rows(squares_of(scaled), first)
    return jnp.concatenate([scaled.astype(jnp.float32), tail], axis=0)


def put_row_side(ref, points, lengths):
    ref[...] = side_of(points, lengths, True).T.astype(jnp.bfloat16)


def put_col_side(ref, points, lengths):
    ref[...] = side_of(points, lengths, False).astype(jnp.bfloat16)


def half_distance(row_ref, col_ref):
    return jnp.dot(row_ref[...], col_ref[...], preferred_element_type=jnp.float32)


def add_product(out_ref, half, weight_ref):
    tile = jnp.exp2(half * LOG2E).astype(jnp.bfloat16)
    out_ref[...] += lax.dot_general(
        weight_ref[...], tile, (((1,), (1,)), ((), ())), preferred_element_type=jnp.float32
    )


def add_all(out_refs, row_refs, segments, held):
    rows = len(out_refs)

    def tiles(sides, blocks, feat, begin, count):
        return [
            (out_refs[row], row_refs[row], sides.at[begin + at], blocks.at[begin + at, feat:])
            for at in range(count)
            for row in range(rows)
        ]

    def run(order, half, last):
        for place, (out_ref, _, _, weight_ref) in enumerate(order):
            if place + 1 < len(order):
                ahead = half_distance(*order[place + 1][1:3])
            else:
                ahead = last()
            add_product(out_ref, half, weight_ref)
            half = ahead

    if sum(segment[0].shape[0] for segment in segments) * rows <= UNROLL:
        order = [tile for segment in segments for tile in tiles(*segment, 0, segment[0].shape[0])]
        run(order, half_distance(*order[0][1:3]), lambda: None)
        return

    for sides, blocks, feat in segments:
        cols = sides.shape[0]
        group = max(at for at in range(1, cols + 1) if cols % at == 0 and at * rows <= max(UNROLL, rows))

        def following(begin):
            held[...] = half_distance(row_refs[0], sides.at[begin])

        def body(index, _):
            order = tiles(sides, blocks, feat, index * group, group)
            run(order, held[...], lambda: following((index + 1) * group))
            return 0

        following(0)
        steps = cols // group
        lax.fori_loop(0, steps - 1, body, 0)
        run(tiles(sides, blocks, feat, (steps - 1) * group, group), held[...], lambda: None)


def pack_kernel(points_ref, direction_ref, out_ref, points_out_ref, wide, sems):
    feat = points_ref.shape[0]
    copies = (
        pltpu.make_async_copy(direction_ref, wide, sems.at[0]),
        pltpu.make_async_copy(points_ref, out_ref.at[:feat], sems.at[1]),
    )
    for copy in copies:
        copy.start()
    copies[0].wait()
    out_ref[feat:] = wide[...].astype(jnp.bfloat16)
    copies[1].wait()
    points_out_ref[...] = out_ref[:feat]


def pair_kernel(own_ref, other_ref, pair_ref):
    pair_ref[0] = own_ref[...]
    pair_ref[1] = other_ref[...]


def put_col_sides(col_side, blocks_ref, feat, lengths):
    for at in range(col_side.shape[0]):
        put_col_side(col_side.at[at], blocks_ref[at, :feat], lengths)


def chip_kernel(peers, feat, lengths_ref, pair_ref, *refs):
    points_refs, out_refs = refs[:peers], refs[peers : 2 * peers + 1]
    row_side, col_side, held = refs[2 * peers + 1 :]
    lengths = lengths_ref[...]
    put_col_sides(col_side, pair_ref, feat, lengths)
    for at, ref in enumerate((pair_ref.at[0, :feat], *points_refs)):
        put_row_side(row_side.at[at], ref[...], lengths)
        out_refs[at][...] = jnp.zeros_like(out_refs[at])
    add_all(
        out_refs,
        [row_side.at[at] for at in range(peers + 1)],
        [(col_side, pair_ref, feat)],
        held,
    )


def across_kernel(feat, lengths_ref, pair_ref, pair_side, points_ref, out_ref, row_side, held):
    put_row_side(row_side, points_ref[...], lengths_ref[...])
    out_ref[...] = jnp.zeros_like(out_ref)
    add_all([out_ref], [row_side], [(pair_side, pair_ref, feat)], held)


def onward_kernel(_, *refs):
    for at, ref in enumerate(refs[:-1]):
        refs[-1][at] = ref[...]


def peers_kernel(feat, lengths_ref, blocks_ref, across_side, near_sides, *refs):
    col_side, held = refs[-2:]
    peers = near_sides.shape[0]
    start_refs, out_refs = refs[:peers], refs[peers:-2]
    put_col_sides(col_side, blocks_ref, feat, lengths_ref[...])
    for start_ref, out_ref in zip(start_refs, out_refs):
        out_ref[...] = start_ref[...]
    add_all(
        out_refs,
        [across_side] + [near_sides.at[at] for at in range(1, peers)],
        [(col_side, blocks_ref, feat)],
        held,
    )


def last_kernel(feat, sides_ref, start_ref, line_ref, line_side, blocks_ref, blocks_side, out_ref, held):
    out_ref[...] = start_ref[...]
    add_all(
        [out_ref], [sides_ref.at[0]], [(line_side, line_ref, feat), (blocks_side, blocks_ref, feat)], held
    )


def cost(pairs):
    return pl.CostEstimate(flops=pairs * 768, bytes_accessed=pairs // 4, transcendentals=pairs)


def scattered_kernel(parts, *refs):
    noise_ref, direction_ref, residual_ref = refs[:3]
    image_ref, sums_ref = refs[3 + parts :]
    direction, residual = direction_ref[...], residual_ref[...]
    image = noise_ref[...] * direction
    for ref in refs[3 : 3 + parts]:
        image = image + ref[...]
    image_ref[...] = image
    sums = (
        jnp.sum(residual * residual, axis=1, keepdims=True),
        jnp.sum(direction * image, axis=1, keepdims=True),
        jnp.sum(residual * image, axis=1, keepdims=True),
        jnp.sum(image * image, axis=1, keepdims=True),
    )
    rhs = direction.shape[0]
    lane = lax.broadcasted_iota(jnp.int32, (rhs, 128), 1)
    right = lax.broadcasted_iota(jnp.int32, (rhs, 128), 0)
    packed = jnp.zeros((rhs, 128), jnp.float32)
    for index, value in enumerate(sums):
        packed = jnp.where(lane == index * rhs + right, value, packed)
    row = jnp.sum(packed, axis=0, keepdims=True)
    sums_ref[...] = jnp.broadcast_to(row[None], sums_ref.shape)


def update_kernel(
    solution_ref, residual_ref, direction_ref, image_ref, sums_ref, new_solution, new_residual, new_direction
):
    direction = direction_ref[...]
    rhs = direction.shape[0]
    row = jnp.sum(sums_ref[...], axis=0)
    lane = lax.broadcasted_iota(jnp.int32, (rhs, 128), 1)
    right = lax.broadcasted_iota(jnp.int32, (rhs, 128), 0)
    norm_old, curvature, mixed, image_norm = (
        jnp.sum(jnp.where(lane == index * rhs + right, row, 0.0), axis=1, keepdims=True)
        for index in range(4)
    )
    step = norm_old / curvature
    norm_new = jnp.maximum(norm_old + step * (step * image_norm - 2.0 * mixed), 0.0)
    updated = residual_ref[...] - step * image_ref[...]
    new_solution[...] = solution_ref[...] + step * direction
    new_residual[...] = updated
    new_direction[...] = updated + (norm_new / norm_old) * direction


def swap(array, devices, mask):
    return lax.ppermute(array, AXES, [(at, at ^ mask) for at in range(devices)])


def local(devices, points, lengths, noise_var, solution, residual, direction):
    f32, bf16 = jnp.float32, jnp.bfloat16
    shape = jax.ShapeDtypeStruct
    feat, width = points.shape
    rhs = direction.shape[0]
    depth = feat + TAIL
    masks = (X + Y, X, Y)
    peers = len(masks)
    line_count = devices // LINE - 1
    tile_pairs = width * width
    held = pltpu.VMEM((width, width), f32)
    partial_shape = shape((rhs, width), f32)
    lengths = lengths[:, None]

    along_x = swap(points, devices, X)
    packed, near = pl.pallas_call(
        pack_kernel,
        out_shape=[shape((feat + rhs, width), bf16), shape((feat, width), bf16)],
        in_specs=[pl.BlockSpec(memory_space=pltpu.HBM)] * 2,
        scratch_shapes=[pltpu.VMEM((rhs, width), f32), pltpu.SemaphoreType.DMA((2,))],
        compiler_params=params(),
    )(
        pltpu.with_memory_space_constraint(points, pltpu.HBM),
        pltpu.with_memory_space_constraint(direction, pltpu.HBM),
    )
    line = [swap(packed, devices, LINE * at) for at in range(1, line_count + 1)]
    along_y = swap(near, devices, Y)
    across = swap(along_x, devices, Y)
    pair = pl.pallas_call(
        pair_kernel, out_shape=shape((2, feat + rhs, width), bf16), compiler_params=params()
    )(packed, swap(packed, devices, CORE))

    own, x_partial, y_partial, near_sides, pair_side = pl.pallas_call(
        functools.partial(chip_kernel, 2, feat),
        out_shape=[partial_shape] * 3
        + [shape((3, width, depth), bf16), shape((2, depth, width), bf16)],
        scratch_shapes=[held],
        compiler_params=params(),
        cost_estimate=cost(tile_pairs // 2),
    )(lengths, pair, along_x, along_y)
    across_partial, across_side = pl.pallas_call(
        functools.partial(across_kernel, feat),
        out_shape=[partial_shape, shape((width, depth), bf16)],
        scratch_shapes=[held],
        compiler_params=params(),
        cost_estimate=cost(tile_pairs // 2),
    )(lengths, pair, pair_side, across)
    for_peers = [across_partial, x_partial, y_partial]
    onward = pl.pallas_call(
        onward_kernel,
        out_shape=shape((line_count, feat + rhs, width), bf16),
        in_specs=[pl.BlockSpec(memory_space=pl.ANY)]
        + [pl.BlockSpec(memory_space=pltpu.VMEM)] * line_count,
        compiler_params=params(),
    )(for_peers[0], *line)
    blocks = swap(onward, devices, CORE)
    sides = []
    for columns in (onward, blocks):
        *for_peers, side = pl.pallas_call(
            functools.partial(peers_kernel, feat),
            out_shape=[partial_shape] * peers + [shape((line_count, depth, width), bf16)],
            scratch_shapes=[held],
            compiler_params=params(),
            cost_estimate=cost(peers * line_count * tile_pairs),
        )(lengths, columns, across_side, near_sides, *for_peers)
        sides.append(side)
    from_peers = [swap(part, devices, mask) for part, mask in zip(for_peers, masks)]
    mine = pl.pallas_call(
        functools.partial(last_kernel, feat),
        out_shape=partial_shape,
        scratch_shapes=[held],
        compiler_params=params(),
        cost_estimate=cost(2 * line_count * tile_pairs),
    )(near_sides, own, onward, sides[0], blocks, sides[1])

    image, sums = pl.pallas_call(
        functools.partial(scattered_kernel, 1 + peers),
        out_shape=[shape((rhs, width), f32), shape((devices, 1, 128), f32)],
        compiler_params=params(),
    )(noise_var[None, :], direction, residual, mine, *from_peers)
    all_sums = lax.all_to_all(sums, AXES, 0, 0, tiled=True)
    return tuple(
        pl.pallas_call(
            update_kernel, out_shape=[shape((rhs, width), f32)] * 3, compiler_params=params()
        )(solution, residual, direction, image, all_sums)
    )


def solution(mesh):
    placed = (
        P(None, AXES),
        P(),
        P(AXES),
        P(None, AXES),
        P(None, AXES),
        P(None, AXES),
    )
    return jax.shard_map(
        functools.partial(local, mesh.shape["row"] * mesh.shape["col"]),
        mesh=mesh,
        in_specs=placed,
        out_specs=(P(None, AXES), P(None, AXES), P(None, AXES)),
        check_vma=False,
    )
```

time: 199 us -> 39.4 us (0.20)
  blocking collectives: 150 us -> 10.9 us
  waiting for transfers between devices: 20.4 us -> 3.86 us
  between operations: 14.1 us -> 0.71 us
  starting transfers between devices: 0.04 us -> 13.1 us
  Pallas kernels: 0 us -> 10.5 us
  matrix products: 8.94 us -> 0 us
  other arithmetic: 4.41 us -> 0 us
    psum x2 -> x0, blocking collectives: 80.4 us -> none  [the longest x1 41 us: local(): lax.psum(jnp.sum(new_residual * new_residual, axis=1), ('row', 'col'))]
    all_gather x3 -> x0, blocking collectives: 69.6 us -> none  [the longest x1 31.9 us: grid_image(): col_scaled = lax.all_gather(scaled, 'row', axis=1, tiled=True)]
    reduce_scatter x1 -> x0, waiting for transfers between devices: 20.3 us -> none  [grid_image(): lax.psum_scatter(partial_value, 'col', scatter_dimension=1, tiled=True)]
    ppermute x0 -> x11, starting transfers between devices: none -> 13.1 us  [swap(): return lax.ppermute(array, AXES, [(at, at ^ mask) for at in range(devices)])]
    all_to_all x0 -> x1, blocking collectives: none -> 10.9 us  [local(): all_sums = lax.all_to_all(sums, AXES, 0, 0, tiled=True)]
    pallas_call x0 -> x10, Pallas kernels: none -> 10.5 us  [the longest x2 4.64 us: local(): pl.pallas_call(functools.partial(peers_kernel, feat), out_shape=[partial_...]
    dot_general x2 -> x0, matrix products: 8.94 us -> none  [one_block(): jnp.dot(part_dir, kernel_tile, preferred_element_type=jnp.float32)]
    ppermute x0 -> x11, waiting for transfers between devices: none -> 3.86 us  [swap(): return lax.ppermute(array, AXES, [(at, at ^ mask) for at in range(devices)])]
  transfers between devices with their start and end apart: 1 -> 11, of which waited for: 1 -> 3; matrix products, arithmetic and copies ran while one was open for 0% -> 0% of each run, Pallas kernels for 0% -> 16%
where the time goes in v1:
time: 39.4 us; the launch traced here: 39.2 us
  starting transfers between devices  13.1 us (33%)
  blocking collectives  10.9 us (28%)
  Pallas kernels  10.5 us (27%)
  waiting for transfers between devices  3.86 us (10%)
  between operations  0.71 us (2%)
    ppermute x11, starting transfers between devices, swap(): return lax.ppermute(array, AXES, [(at, at ^ mask) for at in range(devices)])  13.1 us
    all_to_all x1, blocking collectives, local(): all_sums = lax.all_to_all(sums, AXES, 0, 0, tiled=True)  10.9 us
    pallas_call x2, Pallas kernels, local(): pl.pallas_call(functools.partial(peers_kernel, feat), out_shape=[partial_...  4.64 us
    ppermute x11, waiting for transfers between devices, swap(): return lax.ppermute(array, AXES, [(at, at ^ mask) for at in range(devices)])  3.86 us
    pallas_call x1, Pallas kernels, local(): pl.pallas_call(functools.partial(chip_kernel, 2, feat), out_shape=[partia...  1.75 us
    pallas_call x1, Pallas kernels, local(): pl.pallas_call(functools.partial(last_kernel, feat), out_shape=partial_sh...  1.52 us
    pallas_call x1, Pallas kernels, local(): pl.pallas_call(pack_kernel, out_shape=[shape((feat + rhs, width), bf16),...  0.93 us
  transfers between devices with their start and end apart: 11, of which 3 were waited for; matrix products, arithmetic and copies ran while one was open for 0% of the time, Pallas kernels for 16%

profile of v1, /device:TPU:0, one launch (start us, length us, event | category | flops | bytes accessed | tf_op | source)
XLA Modules:
  0.0 39.2 jit_solution(3290709288045083788)
XLA Ops:
  0.6 0.9 %shard_map.85 = (bf16[80,512]{1,0:T(8,128)(2,1)S(1)}, bf16[64,512]{1,0:T(8,128)(2,1)S(1)}) custom-call(bf16[64,512]{1,0:T(8,128)(2,1)} %points_ref.1, f32[16,512]{1,0:T(8,128)} %direction_ref.3), custom_call_target="tpu_custom_call" | custom-call | tf_op jit(solution)/shard_map/pallas_call | solution.py:259
  1.6 0.5 %collective-permute-start = (bf16[80,512]{1,0:T(8,128)(2,1)S(1)}, bf16[80,512]{1,0:T(8,128)(2,1)S(1)}, u32[]{:S(2)}, u32[]{:S(2)}) collective-permute-start(bf16[80,512]{1,0:T(8,128)(2,1)S(1)} %get-tuple-element.22.own_ref), channel_id=1, source_target_pairs={{0,1},{1,0},{2,3},{3,2},{4,5},{5,4},{6,7},{7,6},{8,9},{9,8},{10,11... | collective-permute-start | bytes 245768 | tf_op jit(solution)/shard_map/ppermute | solution.py:241
  2.1 2.6 %collective-permute-start.1 = (bf16[64,512]{1,0:T(8,128)(2,1)S(1)}, bf16[64,512]{1,0:T(8,128)(2,1)S(1)}, u32[]{:S(2)}, u32[]{:S(2)}) collective-permute-start(bf16[64,512]{1,0:T(8,128)(2,1)S(1)} %copy-done.4), channel_id=1, source_target_pairs={{0,2},{1,3},{2,0},{3,1},{4,6},{5,7},{6,4},{7,5},{8,10},{9,11},{10,... | collective-permute-start | bytes 196616 | tf_op jit(solution)/shard_map/ppermute | solution.py:241
  4.7 1.5 %collective-permute-start.2 = (bf16[64,512]{1,0:T(8,128)(2,1)S(1)}, bf16[64,512]{1,0:T(8,128)(2,1)S(1)}, u32[]{:S(2)}, u32[]{:S(2)}) collective-permute-start(bf16[64,512]{1,0:T(8,128)(2,1)S(1)} %get-tuple-element.23), channel_id=1, source_target_pairs={{0,4},{1,5},{2,6},{3,7},{4,0},{5,1},{6,2},{7,3},{8,12},{9,13},{10,... | collective-permute-start | bytes 196616 | tf_op jit(solution)/shard_map/ppermute | solution.py:241
  6.2 3.6 %collective-permute-start.6 = (bf16[80,512]{1,0:T(8,128)(2,1)S(1)}, bf16[80,512]{1,0:T(8,128)(2,1)S(1)}, u32[]{:S(2)}, u32[]{:S(2)}) collective-permute-start(bf16[80,512]{1,0:T(8,128)(2,1)S(1)} %get-tuple-element.22.own_ref), channel_id=1, source_target_pairs={{0,24},{1,25},{2,26},{3,27},{4,28},{5,29},{6,30},{7,31},{8,16},{9,... | collective-permute-start | bytes 245768 | tf_op jit(solution)/shard_map/ppermute | solution.py:241
  9.8 0.8 %collective-permute-start.4 = (bf16[80,512]{1,0:T(8,128)(2,1)S(1)}, bf16[80,512]{1,0:T(8,128)(2,1)S(1)}, u32[]{:S(2)}, u32[]{:S(2)}) collective-permute-start(bf16[80,512]{1,0:T(8,128)(2,1)S(1)} %get-tuple-element.22.own_ref), channel_id=1, source_target_pairs={{0,8},{1,9},{2,10},{3,11},{4,12},{5,13},{6,14},{7,15},{8,0},{9,1},... | collective-permute-start | bytes 245768 | tf_op jit(solution)/shard_map/ppermute | solution.py:241
  10.6 0.5 %collective-permute-start.3 = (bf16[64,512]{1,0:T(8,128)(2,1)S(1)}, bf16[64,512]{1,0:T(8,128)(2,1)S(1)}, u32[]{:S(2)}, u32[]{:S(2)}) collective-permute-start(bf16[64,512]{1,0:T(8,128)(2,1)S(1)} %collective-permute-done.1.refs_0_), channel_id=1, source_target_pairs={{0,4},{1,5},{2,6},{3,7},{4,0},{5,1},{6,2},{7,3},{8,12},{9,13},{10,... | collective-permute-start | bytes 196616 | tf_op jit(solution)/shard_map/ppermute | solution.py:241
  11.1 0.1 copy.9.lengths_ref
  11.2 1.7 %shard_map.87 = (f32[16,512]{1,0:T(8,128)S(1)}, f32[16,512]{1,0:T(8,128)S(1)}, f32[16,512]{1,0:T(8,128)S(1)}, bf16[3,512,80]{2,1,0:T(8,128)(2,1)S(1)}, bf16[2,80,512]{2,1,0:T(8,128)(2,1)S(1)}) custom-call(f32[64,1]{1,0:T(8,128)S(1)} %copy.9.lengths_ref, bf16[2,80,512]{2,1,0:T(8,128)(2,1)S(1)} %shard_map.86.pair_ref, ...), custom_call_target="tpu_custom_call" | custom-call | flops 100663296 | bytes 32768 | tf_op jit(solution)/shard_map/pallas_call | solution.py:276
  13.0 1.9 %collective-permute-done.3.points_ref = bf16[64,512]{1,0:T(8,128)(2,1)S(1)} collective-permute-done((bf16[64,512]{1,0:T(8,128)(2,1)S(1)}, bf16[64,512]{1,0:T(8,128)(2,1)S(1)}, u32[]{:S(2)}, u32[]{:S(2)}) %collective-permute-start.3) | collective-permute-done | bytes 65568 | tf_op jit(solution)/shard_map/ppermute | solution.py:241
  14.9 0.8 %shard_map.88 = (f32[16,512]{1,0:T(8,128)S(1)}, bf16[512,80]{1,0:T(8,128)(2,1)S(1)}) custom-call(f32[64,1]{1,0:T(8,128)S(1)} %copy.9.lengths_ref, bf16[2,80,512]{2,1,0:T(8,128)(2,1)S(1)} %shard_map.86.pair_ref, bf16[2,80,512]{2,1,0:T(8,128)(2,1)S(1)} %get-tuple-element.26.pair_side, bf16[64,512]{1,0:T(8,128)(2,1)S(1)} %collective-permute-done.3.points_ref), custom_call_target="tpu_custom_call" | custom-call | flops 100663296 | bytes 32768 | tf_op jit(solution)/shard_map/pallas_call | solution.py:284
  15.6 1.1 %collective-permute-done.5.refs_1_ = bf16[80,512]{1,0:T(8,128)(2,1)S(1)} collective-permute-done((bf16[80,512]{1,0:T(8,128)(2,1)S(1)}, bf16[80,512]{1,0:T(8,128)(2,1)S(1)}, u32[]{:S(2)}, u32[]{:S(2)}) %collective-permute-start.5) | collective-permute-done | bytes 81952 | tf_op jit(solution)/shard_map/ppermute | solution.py:241
  16.7 0.1 collective-permute-start.7
  16.8 2.3 %shard_map.90 = (f32[16,512]{1,0:T(8,128)S(1)}, f32[16,512]{1,0:T(8,128)S(1)}, f32[16,512]{1,0:T(8,128)S(1)}, bf16[3,80,512]{2,1,0:T(8,128)(2,1)S(1)}) custom-call(f32[64,1]{1,0:T(8,128)S(1)} %copy.9.lengths_ref, bf16[3,80,512]{2,1,0:T(8,128)(2,1)S(1)} %shard_map.89.blocks_ref.line_ref, bf16[512,80]{1,0:T(8,128)(2,1)S(1)} %get-tuple-element.28.across_side, ...), custom_call_target="tpu_custom_call" | custom-call | flops 1811939328 | bytes 589824 | tf_op jit(solution)/shard_map/pallas_call | solution.py:302
  19.1 2.3 %shard_map.91 = (f32[16,512]{1,0:T(8,128)S(1)}, f32[16,512]{1,0:T(8,128)S(1)}, f32[16,512]{1,0:T(8,128)S(1)}, bf16[3,80,512]{2,1,0:T(8,128)(2,1)S(1)}) custom-call(f32[64,1]{1,0:T(8,128)S(1)} %copy.9.lengths_ref, bf16[3,80,512]{2,1,0:T(8,128)(2,1)S(1)} %collective-permute-done.7.blocks_ref, bf16[512,80]{1,0:T(8,128)(2,1)S(1)} %get-tuple-element.28.across_side, ...), custom_call_target="tpu_custom_call" | custom-call | flops 1811939328 | bytes 589824 | tf_op jit(solution)/shard_map/pallas_call | solution.py:302
  21.4 0.5 %collective-permute-start.8 = (f32[16,512]{1,0:T(8,128)S(1)}, f32[16,512]{1,0:T(8,128)S(1)}, u32[]{:S(2)}, u32[]{:S(2)}) collective-permute-start(f32[16,512]{1,0:T(8,128)S(1)} %get-tuple-element.36), channel_id=1, source_target_pairs={{0,6},{1,7},{2,4},{3,5},{4,2},{5,3},{6,0},{7,1},{8,14},{9,15},{10,... | collective-permute-start | bytes 98312 | tf_op jit(solution)/shard_map/ppermute | solution.py:241
  21.9 1.5 %collective-permute-start.9 = (f32[16,512]{1,0:T(8,128)S(1)}, f32[16,512]{1,0:T(8,128)S(1)}, u32[]{:S(2)}, u32[]{:S(2)}) collective-permute-start(f32[16,512]{1,0:T(8,128)S(1)} %get-tuple-element.37), channel_id=1, source_target_pairs={{0,2},{1,3},{2,0},{3,1},{4,6},{5,7},{6,4},{7,5},{8,10},{9,11},{10,... | collective-permute-start | bytes 98312 | tf_op jit(solution)/shard_map/ppermute | solution.py:241
  23.4 1.5 %collective-permute-start.10 = (f32[16,512]{1,0:T(8,128)S(1)}, f32[16,512]{1,0:T(8,128)S(1)}, u32[]{:S(2)}, u32[]{:S(2)}) collective-permute-start(f32[16,512]{1,0:T(8,128)S(1)} %get-tuple-element.38), channel_id=1, source_target_pairs={{0,4},{1,5},{2,6},{3,7},{4,0},{5,1},{6,2},{7,3},{8,12},{9,13},{10,... | collective-permute-start | bytes 98312 | tf_op jit(solution)/shard_map/ppermute | solution.py:241
  25.0 1.5 %shard_map.92.refs_3_ = f32[16,512]{1,0:T(8,128)S(1)} custom-call(bf16[3,512,80]{2,1,0:T(8,128)(2,1)S(1)} %get-tuple-element.24.near_sides.sides_ref, f32[16,512]{1,0:T(8,128)S(1)} %get-tuple-element.25.start_ref, bf16[3,80,512]{2,1,0:T(8,128)(2,1)S(1)} %shard_map.89.blocks_ref.line_ref, bf16[3,80,512]{2,1,0:T(8,128)(2,1)S(1)} %get-tuple-element.31.line_side, ...), custom_call_target="tpu_custom_call" | custom-call | flops 1207959552 | bytes 393216 | tf_op jit(solution)/shard_map/pallas_call | solution.py:311
  26.5 0.0 collective-permute-done.8.refs_4_
  26.5 0.9 %collective-permute-done.10.refs_6_ = f32[16,512]{1,0:T(8,128)S(1)} collective-permute-done((f32[16,512]{1,0:T(8,128)S(1)}, f32[16,512]{1,0:T(8,128)S(1)}, u32[]{:S(2)}, u32[]{:S(2)}) %collective-permute-start.10) | collective-permute-done | bytes 32800 | tf_op jit(solution)/shard_map/ppermute | solution.py:241
  27.4 0.1 shard_map.93
  27.5 10.9 %all_to_all.5.sums_ref = f32[32,1,128]{2,1,0:T(1,128)S(1)} all-to-all(f32[32,1,128]{2,1,0:T(1,128)S(1)} %get-tuple-element.40), channel_id=1, replica_groups=mesh['row'=8,'col'=4] {'row','col'}, dimensions={0} | all-to-all | bytes 32768 | tf_op jit(solution)/shard_map/all_to_all | solution.py:324
  38.4 0.8 %shard_map.94 = (f32[16,512]{1,0:T(8,128)}, f32[16,512]{1,0:T(8,128)}, f32[16,512]{1,0:T(8,128)}) custom-call(f32[16,512]{1,0:T(8,128)S(1)} %copy-done.2, f32[16,512]{1,0:T(8,128)S(1)} %copy-done.1, f32[16,512]{1,0:T(8,128)S(1)} %copy-done, f32[16,512]{1,0:T(8,128)S(1)} %get-tuple-element.39.image_ref, f32[32,1,128]{2,1,0:T(1,128)S(1)} %all_to_all.5.sums_ref), custom_call_target="tpu_custom_call" | custom-call | tf_op jit(solution)/shard_map/pallas_call | solution.py:326
  (22 shorter events, 0.1 us)
Async XLA Ops:
  0.6 1.5 %copy-start.4 = (bf16[64,512]{1,0:T(8,128)(2,1)S(1)}, bf16[64,512]{1,0:T(8,128)(2,1)}, u32[]{:S(2)}) copy-start(bf16[64,512]{1,0:T(8,128)(2,1)} %points_ref.1) | copy-start | bytes 196612
  1.6 9.0 %collective-permute-start = (bf16[80,512]{1,0:T(8,128)(2,1)S(1)}, bf16[80,512]{1,0:T(8,128)(2,1)S(1)}, u32[]{:S(2)}, u32[]{:S(2)}) collective-permute-start(bf16[80,512]{1,0:T(8,128)(2,1)S(1)} %get-tuple-element.22.own_ref), channel_id=1, source_target_pairs={{0,1},{1,0},{2,3},{3,2},{4,5},{5,4},{6,7},{7,6},{8,9},{9,8},{10,11... | collective-permute-start | bytes 245768 | tf_op jit(solution)/shard_map/ppermute | solution.py:241
  2.1 7.7 %collective-permute-start.1 = (bf16[64,512]{1,0:T(8,128)(2,1)S(1)}, bf16[64,512]{1,0:T(8,128)(2,1)S(1)}, u32[]{:S(2)}, u32[]{:S(2)}) collective-permute-start(bf16[64,512]{1,0:T(8,128)(2,1)S(1)} %copy-done.4), channel_id=1, source_target_pairs={{0,2},{1,3},{2,0},{3,1},{4,6},{5,7},{6,4},{7,5},{8,10},{9,11},{10,... | collective-permute-start | bytes 196616 | tf_op jit(solution)/shard_map/ppermute | solution.py:241
  4.7 6.4 %copy-start.5 = (f32[64]{0:T(128)S(1)}, f32[64]{0:T(128)}, u32[]{:S(2)}) copy-start(f32[64]{0:T(128)} %param.7) | copy-start | bytes 772
  4.7 6.5 %collective-permute-start.2 = (bf16[64,512]{1,0:T(8,128)(2,1)S(1)}, bf16[64,512]{1,0:T(8,128)(2,1)S(1)}, u32[]{:S(2)}, u32[]{:S(2)}) collective-permute-start(bf16[64,512]{1,0:T(8,128)(2,1)S(1)} %get-tuple-element.23), channel_id=1, source_target_pairs={{0,4},{1,5},{2,6},{3,7},{4,0},{5,1},{6,2},{7,3},{8,12},{9,13},{10,... | collective-permute-start | bytes 196616 | tf_op jit(solution)/shard_map/ppermute | solution.py:241
  6.2 9.4 %collective-permute-start.6 = (bf16[80,512]{1,0:T(8,128)(2,1)S(1)}, bf16[80,512]{1,0:T(8,128)(2,1)S(1)}, u32[]{:S(2)}, u32[]{:S(2)}) collective-permute-start(bf16[80,512]{1,0:T(8,128)(2,1)S(1)} %get-tuple-element.22.own_ref), channel_id=1, source_target_pairs={{0,24},{1,25},{2,26},{3,27},{4,28},{5,29},{6,30},{7,31},{8,16},{9,... | collective-permute-start | bytes 245768 | tf_op jit(solution)/shard_map/ppermute | solution.py:241
  9.8 6.9 %collective-permute-start.5 = (bf16[80,512]{1,0:T(8,128)(2,1)S(1)}, bf16[80,512]{1,0:T(8,128)(2,1)S(1)}, u32[]{:S(2)}, u32[]{:S(2)}) collective-permute-start(bf16[80,512]{1,0:T(8,128)(2,1)S(1)} %get-tuple-element.22.own_ref), channel_id=1, source_target_pairs={{0,16},{1,17},{2,18},{3,19},{4,20},{5,21},{6,22},{7,23},{8,24},{9,... | collective-permute-start | bytes 245768 | tf_op jit(solution)/shard_map/ppermute | solution.py:241
  9.8 6.9 %collective-permute-start.4 = (bf16[80,512]{1,0:T(8,128)(2,1)S(1)}, bf16[80,512]{1,0:T(8,128)(2,1)S(1)}, u32[]{:S(2)}, u32[]{:S(2)}) collective-permute-start(bf16[80,512]{1,0:T(8,128)(2,1)S(1)} %get-tuple-element.22.own_ref), channel_id=1, source_target_pairs={{0,8},{1,9},{2,10},{3,11},{4,12},{5,13},{6,14},{7,15},{8,0},{9,1},... | collective-permute-start | bytes 245768 | tf_op jit(solution)/shard_map/ppermute | solution.py:241
  10.6 4.3 %collective-permute-start.3 = (bf16[64,512]{1,0:T(8,128)(2,1)S(1)}, bf16[64,512]{1,0:T(8,128)(2,1)S(1)}, u32[]{:S(2)}, u32[]{:S(2)}) collective-permute-start(bf16[64,512]{1,0:T(8,128)(2,1)S(1)} %collective-permute-done.1.refs_0_), channel_id=1, source_target_pairs={{0,4},{1,5},{2,6},{3,7},{4,0},{5,1},{6,2},{7,3},{8,12},{9,13},{10,... | collective-permute-start | bytes 196616 | tf_op jit(solution)/shard_map/ppermute | solution.py:241
  16.7 2.4 %collective-permute-start.7 = (bf16[3,80,512]{2,1,0:T(8,128)(2,1)S(1)}, bf16[3,80,512]{2,1,0:T(8,128)(2,1)S(1)}, u32[]{:S(2)}, u32[]{:S(2)}) collective-permute-start(bf16[3,80,512]{2,1,0:T(8,128)(2,1)S(1)} %shard_map.89.blocks_ref.line_ref), channel_id=1, source_target_pairs={{0,1},{1,0},{2,3},{3,2},{4,5},{5,4},{6,7},{7,6},{8,9},{9,8},{10,11... | collective-permute-start | bytes 737288 | tf_op jit(solution)/shard_map/ppermute | solution.py:241
  21.4 5.1 %collective-permute-start.8 = (f32[16,512]{1,0:T(8,128)S(1)}, f32[16,512]{1,0:T(8,128)S(1)}, u32[]{:S(2)}, u32[]{:S(2)}) collective-permute-start(f32[16,512]{1,0:T(8,128)S(1)} %get-tuple-element.36), channel_id=1, source_target_pairs={{0,6},{1,7},{2,4},{3,5},{4,2},{5,3},{6,0},{7,1},{8,14},{9,15},{10,... | collective-permute-start | bytes 98312 | tf_op jit(solution)/shard_map/ppermute | solution.py:241
  21.9 4.6 %collective-permute-start.9 = (f32[16,512]{1,0:T(8,128)S(1)}, f32[16,512]{1,0:T(8,128)S(1)}, u32[]{:S(2)}, u32[]{:S(2)}) collective-permute-start(f32[16,512]{1,0:T(8,128)S(1)} %get-tuple-element.37), channel_id=1, source_target_pairs={{0,2},{1,3},{2,0},{3,1},{4,6},{5,7},{6,4},{7,5},{8,10},{9,11},{10,... | collective-permute-start | bytes 98312 | tf_op jit(solution)/shard_map/ppermute | solution.py:241
  23.4 3.9 %collective-permute-start.10 = (f32[16,512]{1,0:T(8,128)S(1)}, f32[16,512]{1,0:T(8,128)S(1)}, u32[]{:S(2)}, u32[]{:S(2)}) collective-permute-start(f32[16,512]{1,0:T(8,128)S(1)} %get-tuple-element.38), channel_id=1, source_target_pairs={{0,4},{1,5},{2,6},{3,7},{4,0},{5,1},{6,2},{7,3},{8,12},{9,13},{10,... | collective-permute-start | bytes 98312 | tf_op jit(solution)/shard_map/ppermute | solution.py:241
  25.0 2.4 %copy-start = (f32[16,512]{1,0:T(8,128)S(1)}, f32[16,512]{1,0:T(8,128)}, u32[]{:S(2)}) copy-start(f32[16,512]{1,0:T(8,128)} %direction_ref.3) | copy-start | bytes 98308
  25.0 2.4 %copy-start.1 = (f32[16,512]{1,0:T(8,128)S(1)}, f32[16,512]{1,0:T(8,128)}, u32[]{:S(2)}) copy-start(f32[16,512]{1,0:T(8,128)} %residual_ref.1) | copy-start | bytes 98308
  25.0 2.4 %copy-start.3 = (f32[512]{0:T(512)S(1)}, f32[512]{0:T(512)}, u32[]{:S(2)}) copy-start(f32[512]{0:T(512)} %param.8) | copy-start | bytes 6148
  27.5 10.9 %copy-start.2 = (f32[16,512]{1,0:T(8,128)S(1)}, f32[16,512]{1,0:T(8,128)}, u32[]{:S(2)}) copy-start(f32[16,512]{1,0:T(8,128)} %solution_ref.1) | copy-start | bytes 98308

commit v2 on v1

--- a/solution.py
+++ b/solution.py
@@ -241,6 +241,12 @@
     return lax.ppermute(array, AXES, [(at, at ^ mask) for at in range(devices)])
 
 
+def shift_line(array, devices, steps):
+    return lax.ppermute(
+        array, AXES, [(at, (at + steps * LINE) % devices) for at in range(devices)]
+    )
+
+
 def local(devices, points, lengths, noise_var, solution, residual, direction):
     f32, bf16 = jnp.float32, jnp.bfloat16
     shape = jax.ShapeDtypeStruct
@@ -266,7 +272,7 @@
         pltpu.with_memory_space_constraint(points, pltpu.HBM),
         pltpu.with_memory_space_constraint(direction, pltpu.HBM),
     )
-    line = [swap(packed, devices, LINE * at) for at in range(1, line_count + 1)]
+    line = [shift_line(packed, devices, steps) for steps in range(line_count, 0, -1)]
     along_y = swap(near, devices, Y)
     across = swap(along_x, devices, Y)
     pair = pl.pallas_call(

time: 39.4 us -> 39.4 us (level)
  starting transfers between devices: 13.1 us -> 14.7 us
  waiting for transfers between devices: 3.86 us -> 2.79 us
  blocking collectives: 10.9 us -> 10.3 us
    ppermute x0 -> x3, starting transfers between devices: none -> 5.51 us  [shift_line(): lax.ppermute(array, AXES, [(at, (at + steps * LINE) % devices) for at in...]
    ppermute x11 -> x8, starting transfers between devices: 13.1 us -> 9.21 us  [swap(): return lax.ppermute(array, AXES, [(at, at ^ mask) for at in range(devices)])]
    ppermute x11 -> x8, waiting for transfers between devices: 3.86 us -> 2.75 us  [swap(): return lax.ppermute(array, AXES, [(at, at ^ mask) for at in range(devices)])]
    all_to_all x1, blocking collectives: 10.9 us -> 10.3 us  [local(): all_sums = lax.all_to_all(sums, AXES, 0, 0, tiled=True)]
where the time goes in v2:
time: 39.4 us; the launch traced here: 39.2 us
  starting transfers between devices  14.7 us (37%)
  Pallas kernels  10.5 us (27%)
  blocking collectives  10.3 us (26%)
  waiting for transfers between devices  2.79 us (7%)
  between operations  0.72 us (2%)
    all_to_all x1, blocking collectives, local(): all_sums = lax.all_to_all(sums, AXES, 0, 0, tiled=True)  10.3 us
    ppermute x8, starting transfers between devices, swap(): return lax.ppermute(array, AXES, [(at, at ^ mask) for at in range(devices)])  9.21 us
    ppermute x3, starting transfers between devices, shift_line(): lax.ppermute(array, AXES, [(at, (at + steps * LINE) % devices) for at in...  5.51 us
    pallas_call x2, Pallas kernels, local(): pl.pallas_call(functools.partial(peers_kernel, feat), out_shape=[partial_...  4.65 us
    ppermute x8, waiting for transfers between devices, swap(): return lax.ppermute(array, AXES, [(at, at ^ mask) for at in range(devices)])  2.75 us
    pallas_call x1, Pallas kernels, local(): pl.pallas_call(functools.partial(chip_kernel, 2, feat), out_shape=[partia...  1.75 us
    pallas_call x1, Pallas kernels, local(): pl.pallas_call(functools.partial(last_kernel, feat), out_shape=partial_sh...  1.52 us
    pallas_call x1, Pallas kernels, local(): pl.pallas_call(pack_kernel, out_shape=[shape((feat + rhs, width), bf16),...  0.93 us
  transfers between devices with their start and end apart: 11, of which 3 were waited for; matrix products, arithmetic and copies ran while one was open for 0% of the time, Pallas kernels for 16%

profile of v2, /device:TPU:0, one launch (start us, length us, event | category | flops | bytes accessed | tf_op | source)
XLA Modules:
  0.0 39.2 jit_solution(4518701598697724232)
XLA Ops:
  0.6 0.9 %shard_map.85 = (bf16[80,512]{1,0:T(8,128)(2,1)S(1)}, bf16[64,512]{1,0:T(8,128)(2,1)S(1)}) custom-call(bf16[64,512]{1,0:T(8,128)(2,1)} %points_ref.1, f32[16,512]{1,0:T(8,128)} %direction_ref.3), custom_call_target="tpu_custom_call" | custom-call | tf_op jit(solution)/shard_map/pallas_call | solution.py:265
  1.6 0.5 %collective-permute-start = (bf16[80,512]{1,0:T(8,128)(2,1)S(1)}, bf16[80,512]{1,0:T(8,128)(2,1)S(1)}, u32[]{:S(2)}, u32[]{:S(2)}) collective-permute-start(bf16[80,512]{1,0:T(8,128)(2,1)S(1)} %get-tuple-element.22.own_ref), channel_id=1, source_target_pairs={{0,1},{1,0},{2,3},{3,2},{4,5},{5,4},{6,7},{7,6},{8,9},{9,8},{10,11... | collective-permute-start | bytes 245768 | tf_op jit(solution)/shard_map/ppermute | solution.py:241
  2.1 2.6 %collective-permute-start.1 = (bf16[64,512]{1,0:T(8,128)(2,1)S(1)}, bf16[64,512]{1,0:T(8,128)(2,1)S(1)}, u32[]{:S(2)}, u32[]{:S(2)}) collective-permute-start(bf16[64,512]{1,0:T(8,128)(2,1)S(1)} %copy-done.4), channel_id=1, source_target_pairs={{0,2},{1,3},{2,0},{3,1},{4,6},{5,7},{6,4},{7,5},{8,10},{9,11},{10,... | collective-permute-start | bytes 196616 | tf_op jit(solution)/shard_map/ppermute | solution.py:241
  4.7 1.5 %collective-permute-start.2 = (bf16[64,512]{1,0:T(8,128)(2,1)S(1)}, bf16[64,512]{1,0:T(8,128)(2,1)S(1)}, u32[]{:S(2)}, u32[]{:S(2)}) collective-permute-start(bf16[64,512]{1,0:T(8,128)(2,1)S(1)} %get-tuple-element.23), channel_id=1, source_target_pairs={{0,4},{1,5},{2,6},{3,7},{4,0},{5,1},{6,2},{7,3},{8,12},{9,13},{10,... | collective-permute-start | bytes 196616 | tf_op jit(solution)/shard_map/ppermute | solution.py:241
  6.2 1.6 %collective-permute-start.6 = (bf16[80,512]{1,0:T(8,128)(2,1)S(1)}, bf16[80,512]{1,0:T(8,128)(2,1)S(1)}, u32[]{:S(2)}, u32[]{:S(2)}) collective-permute-start(bf16[80,512]{1,0:T(8,128)(2,1)S(1)} %get-tuple-element.22.own_ref), channel_id=1, source_target_pairs={{0,8},{1,9},{2,10},{3,11},{4,12},{5,13},{6,14},{7,15},{8,16},{9,17... | collective-permute-start | bytes 245768 | tf_op jit(solution)/shard_map/ppermute | solution.py:245
  7.8 2.6 %collective-permute-start.5 = (bf16[80,512]{1,0:T(8,128)(2,1)S(1)}, bf16[80,512]{1,0:T(8,128)(2,1)S(1)}, u32[]{:S(2)}, u32[]{:S(2)}) collective-permute-start(bf16[80,512]{1,0:T(8,128)(2,1)S(1)} %get-tuple-element.22.own_ref), channel_id=1, source_target_pairs={{0,16},{1,17},{2,18},{3,19},{4,20},{5,21},{6,22},{7,23},{8,24},{9,... | collective-permute-start | bytes 245768 | tf_op jit(solution)/shard_map/ppermute | solution.py:245
  10.4 1.3 %collective-permute-start.4 = (bf16[80,512]{1,0:T(8,128)(2,1)S(1)}, bf16[80,512]{1,0:T(8,128)(2,1)S(1)}, u32[]{:S(2)}, u32[]{:S(2)}) collective-permute-start(bf16[80,512]{1,0:T(8,128)(2,1)S(1)} %get-tuple-element.22.own_ref), channel_id=1, source_target_pairs={{0,24},{1,25},{2,26},{3,27},{4,28},{5,29},{6,30},{7,31},{8,0},{9,1... | collective-permute-start | bytes 245768 | tf_op jit(solution)/shard_map/ppermute | solution.py:245
  11.7 1.0 %collective-permute-start.3 = (bf16[64,512]{1,0:T(8,128)(2,1)S(1)}, bf16[64,512]{1,0:T(8,128)(2,1)S(1)}, u32[]{:S(2)}, u32[]{:S(2)}) collective-permute-start(bf16[64,512]{1,0:T(8,128)(2,1)S(1)} %collective-permute-done.1.refs_0_), channel_id=1, source_target_pairs={{0,4},{1,5},{2,6},{3,7},{4,0},{5,1},{6,2},{7,3},{8,12},{9,13},{10,... | collective-permute-start | bytes 196616 | tf_op jit(solution)/shard_map/ppermute | solution.py:241
  12.7 0.1 copy.9.lengths_ref
  12.9 1.7 %shard_map.87 = (f32[16,512]{1,0:T(8,128)S(1)}, f32[16,512]{1,0:T(8,128)S(1)}, f32[16,512]{1,0:T(8,128)S(1)}, bf16[3,512,80]{2,1,0:T(8,128)(2,1)S(1)}, bf16[2,80,512]{2,1,0:T(8,128)(2,1)S(1)}) custom-call(f32[64,1]{1,0:T(8,128)S(1)} %copy.9.lengths_ref, bf16[2,80,512]{2,1,0:T(8,128)(2,1)S(1)} %shard_map.86.pair_ref, ...), custom_call_target="tpu_custom_call" | custom-call | flops 100663296 | bytes 32768 | tf_op jit(solution)/shard_map/pallas_call | solution.py:282
  14.6 1.4 %collective-permute-done.3.points_ref = bf16[64,512]{1,0:T(8,128)(2,1)S(1)} collective-permute-done((bf16[64,512]{1,0:T(8,128)(2,1)S(1)}, bf16[64,512]{1,0:T(8,128)(2,1)S(1)}, u32[]{:S(2)}, u32[]{:S(2)}) %collective-permute-start.3) | collective-permute-done | bytes 65568 | tf_op jit(solution)/shard_map/ppermute | solution.py:241
  16.0 0.8 %shard_map.88 = (f32[16,512]{1,0:T(8,128)S(1)}, bf16[512,80]{1,0:T(8,128)(2,1)S(1)}) custom-call(f32[64,1]{1,0:T(8,128)S(1)} %copy.9.lengths_ref, bf16[2,80,512]{2,1,0:T(8,128)(2,1)S(1)} %shard_map.86.pair_ref, bf16[2,80,512]{2,1,0:T(8,128)(2,1)S(1)} %get-tuple-element.26.pair_side, bf16[64,512]{1,0:T(8,128)(2,1)S(1)} %collective-permute-done.3.points_ref), custom_call_target="tpu_custom_call" | custom-call | flops 100663296 | bytes 32768 | tf_op jit(solution)/shard_map/pallas_call | solution.py:290
  16.8 0.1 collective-permute-start.7
  16.9 2.3 %shard_map.90 = (f32[16,512]{1,0:T(8,128)S(1)}, f32[16,512]{1,0:T(8,128)S(1)}, f32[16,512]{1,0:T(8,128)S(1)}, bf16[3,80,512]{2,1,0:T(8,128)(2,1)S(1)}) custom-call(f32[64,1]{1,0:T(8,128)S(1)} %copy.9.lengths_ref, bf16[3,80,512]{2,1,0:T(8,128)(2,1)S(1)} %shard_map.89.blocks_ref.line_ref, bf16[512,80]{1,0:T(8,128)(2,1)S(1)} %get-tuple-element.28.across_side, ...), custom_call_target="tpu_custom_call" | custom-call | flops 1811939328 | bytes 589824 | tf_op jit(solution)/shard_map/pallas_call | solution.py:308
  19.2 2.3 %shard_map.91 = (f32[16,512]{1,0:T(8,128)S(1)}, f32[16,512]{1,0:T(8,128)S(1)}, f32[16,512]{1,0:T(8,128)S(1)}, bf16[3,80,512]{2,1,0:T(8,128)(2,1)S(1)}) custom-call(f32[64,1]{1,0:T(8,128)S(1)} %copy.9.lengths_ref, bf16[3,80,512]{2,1,0:T(8,128)(2,1)S(1)} %collective-permute-done.7.blocks_ref, bf16[512,80]{1,0:T(8,128)(2,1)S(1)} %get-tuple-element.28.across_side, ...), custom_call_target="tpu_custom_call" | custom-call | flops 1811939328 | bytes 589824 | tf_op jit(solution)/shard_map/pallas_call | solution.py:308
  21.5 2.0 %collective-permute-start.8 = (f32[16,512]{1,0:T(8,128)S(1)}, f32[16,512]{1,0:T(8,128)S(1)}, u32[]{:S(2)}, u32[]{:S(2)}) collective-permute-start(f32[16,512]{1,0:T(8,128)S(1)} %get-tuple-element.36), channel_id=1, source_target_pairs={{0,6},{1,7},{2,4},{3,5},{4,2},{5,3},{6,0},{7,1},{8,14},{9,15},{10,... | collective-permute-start | bytes 98312 | tf_op jit(solution)/shard_map/ppermute | solution.py:241
  23.5 0.5 %collective-permute-start.9 = (f32[16,512]{1,0:T(8,128)S(1)}, f32[16,512]{1,0:T(8,128)S(1)}, u32[]{:S(2)}, u32[]{:S(2)}) collective-permute-start(f32[16,512]{1,0:T(8,128)S(1)} %get-tuple-element.37), channel_id=1, source_target_pairs={{0,2},{1,3},{2,0},{3,1},{4,6},{5,7},{6,4},{7,5},{8,10},{9,11},{10,... | collective-permute-start | bytes 98312 | tf_op jit(solution)/shard_map/ppermute | solution.py:241
  24.0 1.0 %collective-permute-start.10 = (f32[16,512]{1,0:T(8,128)S(1)}, f32[16,512]{1,0:T(8,128)S(1)}, u32[]{:S(2)}, u32[]{:S(2)}) collective-permute-start(f32[16,512]{1,0:T(8,128)S(1)} %get-tuple-element.38), channel_id=1, source_target_pairs={{0,4},{1,5},{2,6},{3,7},{4,0},{5,1},{6,2},{7,3},{8,12},{9,13},{10,... | collective-permute-start | bytes 98312 | tf_op jit(solution)/shard_map/ppermute | solution.py:241
  25.1 1.5 %shard_map.92.refs_3_ = f32[16,512]{1,0:T(8,128)S(1)} custom-call(bf16[3,512,80]{2,1,0:T(8,128)(2,1)S(1)} %get-tuple-element.24.near_sides.sides_ref, f32[16,512]{1,0:T(8,128)S(1)} %get-tuple-element.25.start_ref, bf16[3,80,512]{2,1,0:T(8,128)(2,1)S(1)} %shard_map.89.blocks_ref.line_ref, bf16[3,80,512]{2,1,0:T(8,128)(2,1)S(1)} %get-tuple-element.31.line_side, ...), custom_call_target="tpu_custom_call" | custom-call | flops 1207959552 | bytes 393216 | tf_op jit(solution)/shard_map/pallas_call | solution.py:317
  26.6 0.8 %collective-permute-done.9.refs_5_ = f32[16,512]{1,0:T(8,128)S(1)} collective-permute-done((f32[16,512]{1,0:T(8,128)S(1)}, f32[16,512]{1,0:T(8,128)S(1)}, u32[]{:S(2)}, u32[]{:S(2)}) %collective-permute-start.9) | collective-permute-done | bytes 32800 | tf_op jit(solution)/shard_map/ppermute | solution.py:241
  27.4 0.5 %collective-permute-done.10.refs_6_ = f32[16,512]{1,0:T(8,128)S(1)} collective-permute-done((f32[16,512]{1,0:T(8,128)S(1)}, f32[16,512]{1,0:T(8,128)S(1)}, u32[]{:S(2)}, u32[]{:S(2)}) %collective-permute-start.10) | collective-permute-done | bytes 32800 | tf_op jit(solution)/shard_map/ppermute | solution.py:241
  28.0 0.1 shard_map.93
  28.1 10.3 %all_to_all.5.sums_ref = f32[32,1,128]{2,1,0:T(1,128)S(1)} all-to-all(f32[32,1,128]{2,1,0:T(1,128)S(1)} %get-tuple-element.40), channel_id=1, replica_groups=mesh['row'=8,'col'=4] {'row','col'}, dimensions={0} | all-to-all | bytes 32768 | tf_op jit(solution)/shard_map/all_to_all | solution.py:330
  38.4 0.8 %shard_map.94 = (f32[16,512]{1,0:T(8,128)}, f32[16,512]{1,0:T(8,128)}, f32[16,512]{1,0:T(8,128)}) custom-call(f32[16,512]{1,0:T(8,128)S(1)} %copy-done.2, f32[16,512]{1,0:T(8,128)S(1)} %copy-done.1, f32[16,512]{1,0:T(8,128)S(1)} %copy-done, f32[16,512]{1,0:T(8,128)S(1)} %get-tuple-element.39.image_ref, f32[32,1,128]{2,1,0:T(1,128)S(1)} %all_to_all.5.sums_ref), custom_call_target="tpu_custom_call" | custom-call | tf_op jit(solution)/shard_map/pallas_call | solution.py:332
  (22 shorter events, 0.1 us)
Async XLA Ops:
  0.6 1.5 %copy-start.4 = (bf16[64,512]{1,0:T(8,128)(2,1)S(1)}, bf16[64,512]{1,0:T(8,128)(2,1)}, u32[]{:S(2)}) copy-start(bf16[64,512]{1,0:T(8,128)(2,1)} %points_ref.1) | copy-start | bytes 196612
  1.6 10.1 %collective-permute-start = (bf16[80,512]{1,0:T(8,128)(2,1)S(1)}, bf16[80,512]{1,0:T(8,128)(2,1)S(1)}, u32[]{:S(2)}, u32[]{:S(2)}) collective-permute-start(bf16[80,512]{1,0:T(8,128)(2,1)S(1)} %get-tuple-element.22.own_ref), channel_id=1, source_target_pairs={{0,1},{1,0},{2,3},{3,2},{4,5},{5,4},{6,7},{7,6},{8,9},{9,8},{10,11... | collective-permute-start | bytes 245768 | tf_op jit(solution)/shard_map/ppermute | solution.py:241
  2.1 8.3 %collective-permute-start.1 = (bf16[64,512]{1,0:T(8,128)(2,1)S(1)}, bf16[64,512]{1,0:T(8,128)(2,1)S(1)}, u32[]{:S(2)}, u32[]{:S(2)}) collective-permute-start(bf16[64,512]{1,0:T(8,128)(2,1)S(1)} %copy-done.4), channel_id=1, source_target_pairs={{0,2},{1,3},{2,0},{3,1},{4,6},{5,7},{6,4},{7,5},{8,10},{9,11},{10,... | collective-permute-start | bytes 196616 | tf_op jit(solution)/shard_map/ppermute | solution.py:241
  4.7 8.1 %copy-start.5 = (f32[64]{0:T(128)S(1)}, f32[64]{0:T(128)}, u32[]{:S(2)}) copy-start(f32[64]{0:T(128)} %param.7) | copy-start | bytes 772
  4.7 8.2 %collective-permute-start.2 = (bf16[64,512]{1,0:T(8,128)(2,1)S(1)}, bf16[64,512]{1,0:T(8,128)(2,1)S(1)}, u32[]{:S(2)}, u32[]{:S(2)}) collective-permute-start(bf16[64,512]{1,0:T(8,128)(2,1)S(1)} %get-tuple-element.23), channel_id=1, source_target_pairs={{0,4},{1,5},{2,6},{3,7},{4,0},{5,1},{6,2},{7,3},{8,12},{9,13},{10,... | collective-permute-start | bytes 196616 | tf_op jit(solution)/shard_map/ppermute | solution.py:241
  6.2 10.6 %collective-permute-start.6 = (bf16[80,512]{1,0:T(8,128)(2,1)S(1)}, bf16[80,512]{1,0:T(8,128)(2,1)S(1)}, u32[]{:S(2)}, u32[]{:S(2)}) collective-permute-start(bf16[80,512]{1,0:T(8,128)(2,1)S(1)} %get-tuple-element.22.own_ref), channel_id=1, source_target_pairs={{0,8},{1,9},{2,10},{3,11},{4,12},{5,13},{6,14},{7,15},{8,16},{9,17... | collective-permute-start | bytes 245768 | tf_op jit(solution)/shard_map/ppermute | solution.py:245
  7.8 9.0 %collective-permute-start.5 = (bf16[80,512]{1,0:T(8,128)(2,1)S(1)}, bf16[80,512]{1,0:T(8,128)(2,1)S(1)}, u32[]{:S(2)}, u32[]{:S(2)}) collective-permute-start(bf16[80,512]{1,0:T(8,128)(2,1)S(1)} %get-tuple-element.22.own_ref), channel_id=1, source_target_pairs={{0,16},{1,17},{2,18},{3,19},{4,20},{5,21},{6,22},{7,23},{8,24},{9,... | collective-permute-start | bytes 245768 | tf_op jit(solution)/shard_map/ppermute | solution.py:245
  10.4 6.4 %collective-permute-start.4 = (bf16[80,512]{1,0:T(8,128)(2,1)S(1)}, bf16[80,512]{1,0:T(8,128)(2,1)S(1)}, u32[]{:S(2)}, u32[]{:S(2)}) collective-permute-start(bf16[80,512]{1,0:T(8,128)(2,1)S(1)} %get-tuple-element.22.own_ref), channel_id=1, source_target_pairs={{0,24},{1,25},{2,26},{3,27},{4,28},{5,29},{6,30},{7,31},{8,0},{9,1... | collective-permute-start | bytes 245768 | tf_op jit(solution)/shard_map/ppermute | solution.py:245
  11.7 4.3 %collective-permute-start.3 = (bf16[64,512]{1,0:T(8,128)(2,1)S(1)}, bf16[64,512]{1,0:T(8,128)(2,1)S(1)}, u32[]{:S(2)}, u32[]{:S(2)}) collective-permute-start(bf16[64,512]{1,0:T(8,128)(2,1)S(1)} %collective-permute-done.1.refs_0_), channel_id=1, source_target_pairs={{0,4},{1,5},{2,6},{3,7},{4,0},{5,1},{6,2},{7,3},{8,12},{9,13},{10,... | collective-permute-start | bytes 196616 | tf_op jit(solution)/shard_map/ppermute | solution.py:241
  16.8 2.4 %collective-permute-start.7 = (bf16[3,80,512]{2,1,0:T(8,128)(2,1)S(1)}, bf16[3,80,512]{2,1,0:T(8,128)(2,1)S(1)}, u32[]{:S(2)}, u32[]{:S(2)}) collective-permute-start(bf16[3,80,512]{2,1,0:T(8,128)(2,1)S(1)} %shard_map.89.blocks_ref.line_ref), channel_id=1, source_target_pairs={{0,1},{1,0},{2,3},{3,2},{4,5},{5,4},{6,7},{7,6},{8,9},{9,8},{10,11... | collective-permute-start | bytes 737288 | tf_op jit(solution)/shard_map/ppermute | solution.py:241
  21.5 5.0 %collective-permute-start.8 = (f32[16,512]{1,0:T(8,128)S(1)}, f32[16,512]{1,0:T(8,128)S(1)}, u32[]{:S(2)}, u32[]{:S(2)}) collective-permute-start(f32[16,512]{1,0:T(8,128)S(1)} %get-tuple-element.36), channel_id=1, source_target_pairs={{0,6},{1,7},{2,4},{3,5},{4,2},{5,3},{6,0},{7,1},{8,14},{9,15},{10,... | collective-permute-start | bytes 98312 | tf_op jit(solution)/shard_map/ppermute | solution.py:241
  23.5 3.9 %collective-permute-start.9 = (f32[16,512]{1,0:T(8,128)S(1)}, f32[16,512]{1,0:T(8,128)S(1)}, u32[]{:S(2)}, u32[]{:S(2)}) collective-permute-start(f32[16,512]{1,0:T(8,128)S(1)} %get-tuple-element.37), channel_id=1, source_target_pairs={{0,2},{1,3},{2,0},{3,1},{4,6},{5,7},{6,4},{7,5},{8,10},{9,11},{10,... | collective-permute-start | bytes 98312 | tf_op jit(solution)/shard_map/ppermute | solution.py:241
  24.0 3.9 %collective-permute-start.10 = (f32[16,512]{1,0:T(8,128)S(1)}, f32[16,512]{1,0:T(8,128)S(1)}, u32[]{:S(2)}, u32[]{:S(2)}) collective-permute-start(f32[16,512]{1,0:T(8,128)S(1)} %get-tuple-element.38), channel_id=1, source_target_pairs={{0,4},{1,5},{2,6},{3,7},{4,0},{5,1},{6,2},{7,3},{8,12},{9,13},{10,... | collective-permute-start | bytes 98312 | tf_op jit(solution)/shard_map/ppermute | solution.py:241
  25.0 2.9 %copy-start = (f32[16,512]{1,0:T(8,128)S(1)}, f32[16,512]{1,0:T(8,128)}, u32[]{:S(2)}) copy-start(f32[16,512]{1,0:T(8,128)} %direction_ref.3) | copy-start | bytes 98308
  25.0 2.9 %copy-start.1 = (f32[16,512]{1,0:T(8,128)S(1)}, f32[16,512]{1,0:T(8,128)}, u32[]{:S(2)}) copy-start(f32[16,512]{1,0:T(8,128)} %residual_ref.1) | copy-start | bytes 98308
  25.1 2.9 %copy-start.3 = (f32[512]{0:T(512)S(1)}, f32[512]{0:T(512)}, u32[]{:S(2)}) copy-start(f32[512]{0:T(512)} %param.8) | copy-start | bytes 6148
  28.1 10.3 %copy-start.2 = (f32[16,512]{1,0:T(8,128)S(1)}, f32[16,512]{1,0:T(8,128)}, u32[]{:S(2)}) copy-start(f32[16,512]{1,0:T(8,128)} %solution_ref.1) | copy-start | bytes 98308

commit v3 on v2

v3 whole, which is shorter than its diff:
```python
import functools
from typing import Any, NamedTuple

import jax
import jax.numpy as jnp
from jax import lax
from jax.experimental import pallas as pl
from jax.experimental.pallas import tpu as pltpu
from jax.sharding import PartitionSpec as P

AXES = ("row", "col")
X, Y = 2, 4
CORE = 1
LINE = 8
LOG2E = 1.4426950408889634
TAIL = 16
UNROLL = 16
EARLY, LATE = 0.25, 6
VMEM_LIMIT = 24 * 1024 * 1024


def params():
    return pltpu.CompilerParams(vmem_limit_bytes=VMEM_LIMIT)


def three_pieces(value):
    high = value.astype(jnp.bfloat16).astype(jnp.float32)
    rest = value - high
    middle = rest.astype(jnp.bfloat16).astype(jnp.float32)
    return high, middle, rest - middle


def tail_rows(squares, first):
    count = squares.shape[1]
    high, middle, low = three_pieces(-0.5 * squares)
    at = lax.broadcasted_iota(jnp.int32, (TAIL, count), 0)
    start = 0 if first else 3
    tail = jnp.where(at < 6, 1.0, 0.0)
    tail = jnp.where(at == start, high, tail)
    tail = jnp.where(at == start + 1, middle, tail)
    tail = jnp.where(at == start + 2, low, tail)
    return tail


def scaled_of(points, lengths):
    return (points.astype(jnp.float32) / lengths).astype(jnp.bfloat16)


def squares_of(scaled):
    values = scaled.astype(jnp.float32)
    return jnp.sum(values * values, axis=0, keepdims=True)


def side_of(points, lengths, first):
    scaled = scaled_of(points, lengths)
    tail = tail_rows(squares_of(scaled), first)
    return jnp.concatenate([scaled.astype(jnp.float32), tail], axis=0)


def put_row_side(ref, points, lengths):
    ref[...] = side_of(points, lengths, True).T.astype(jnp.bfloat16)


def put_col_side(ref, points, lengths):
    ref[...] = side_of(points, lengths, False).astype(jnp.bfloat16)


def half_distance(row_ref, col_ref):
    return jnp.dot(row_ref[...], col_ref[...], preferred_element_type=jnp.float32)


def add_product(out_ref, half, weight_ref):
    tile = jnp.exp2(half * LOG2E).astype(jnp.bfloat16)
    out_ref[...] += lax.dot_general(
        weight_ref[...], tile, (((1,), (1,)), ((), ())), preferred_element_type=jnp.float32
    )


def add_all(groups, feat, held):
    def tiles(rows, sides, blocks, begin, count):
        return [
            (out_ref, row_ref, sides.at[begin + at], blocks.at[begin + at, feat:])
            for at in range(count)
            for out_ref, row_ref in rows
        ]

    def run(order, half, last):
        for place, (out_ref, _, _, weight_ref) in enumerate(order):
            if place + 1 < len(order):
                ahead = half_distance(*order[place + 1][1:3])
            else:
                ahead = last()
            add_product(out_ref, half, weight_ref)
            half = ahead

    pieces = [(rows, sides, blocks) for rows, cols in groups for sides, blocks in cols]
    if sum(len(rows) * sides.shape[0] for rows, sides, _ in pieces) <= UNROLL:
        order = [tile for piece in pieces for tile in tiles(*piece, 0, piece[1].shape[0])]
        run(order, half_distance(*order[0][1:3]), lambda: None)
        return

    for rows, sides, blocks in pieces:
        cols = sides.shape[0]
        group = max(
            at for at in range(1, cols + 1) if cols % at == 0 and (at == 1 or at * len(rows) <= UNROLL)
        )

        def following(begin):
            held[...] = half_distance(rows[0][1], sides.at[begin])

        def body(index, _):
            order = tiles(rows, sides, blocks, index * group, group)
            run(order, held[...], lambda: following((index + 1) * group))
            return 0

        following(0)
        steps = cols // group
        lax.fori_loop(0, steps - 1, body, 0)
        run(tiles(rows, sides, blocks, (steps - 1) * group, group), held[...], lambda: None)


def pack_kernel(points_ref, direction_ref, out_ref, wide, sems):
    feat = points_ref.shape[0]
    copies = (
        pltpu.make_async_copy(direction_ref, wide, sems.at[0]),
        pltpu.make_async_copy(points_ref, out_ref.at[:feat], sems.at[1]),
    )
    for copy in copies:
        copy.start()
    copies[0].wait()
    out_ref[feat:] = wide[...].astype(jnp.bfloat16)
    copies[1].wait()


def pair_kernel(own_ref, other_ref, pair_ref, points_ref):
    pair_ref[0] = own_ref[...]
    pair_ref[1] = other_ref[...]
    points_ref[...] = own_ref[: points_ref.shape[0]]


def after_kernel(_, *refs):
    for at, ref in enumerate(refs[:-1]):
        refs[-1][at] = ref[...]


def after(before, *blocks):
    return pl.pallas_call(
        after_kernel,
        out_shape=jax.ShapeDtypeStruct((len(blocks), *blocks[0].shape), blocks[0].dtype),
        in_specs=[pl.BlockSpec(memory_space=pl.ANY)]
        + [pl.BlockSpec(memory_space=pltpu.VMEM)] * len(blocks),
        compiler_params=params(),
    )(before, *blocks)


class Row(NamedTuple):
    points: Any
    side: Any = None
    partial: Any = None


class Cols(NamedTuple):
    blocks: Any
    sides: Any = None


def products_kernel(feat, new_rows, begun, new_cols, groups, *refs):
    refs = list(refs)

    def take(count):
        taken = refs[:count]
        del refs[:count]
        return taken

    lengths = take(1)[0][...]
    sources, starts = take(len(new_rows)), take(sum(begun))
    blocks, given = take(len(new_cols)), take(len(new_cols) - sum(new_cols))
    outs, made_rows, made_cols = take(len(new_rows)), take(sum(new_rows)), take(sum(new_cols))
    held = refs[0]
    row_sides, col_sides = [], []
    for is_new, block_ref in zip(new_cols, blocks):
        if not is_new:
            col_sides.append(given.pop(0))
            continue
        col_sides.append(made_cols.pop(0))
        for at in range(block_ref.shape[0]):
            put_col_side(col_sides[-1].at[at], block_ref[at, :feat], lengths)
    for is_new, source in zip(new_rows, sources):
        row_sides.append(made_rows.pop(0) if is_new else source)
        if is_new:
            put_row_side(row_sides[-1], source[:feat], lengths)
    for has_start, out_ref in zip(begun, outs):
        out_ref[...] = starts.pop(0)[...] if has_start else jnp.zeros_like(out_ref)
    add_all(
        [
            (
                [(outs[at], row_sides[at]) for at in rows],
                [(col_sides[at], blocks[at]) for at in cols],
            )
            for rows, cols in groups
        ],
        feat,
        held,
    )


def products(lengths, rhs, rows, cols, groups, weight):
    feat, width = lengths.shape[0], cols[0].blocks.shape[2]
    shape = jax.ShapeDtypeStruct
    new_rows = [row.side is None for row in rows]
    begun = [row.partial is not None for row in rows]
    new_cols = [col.sides is None for col in cols]
    depth = feat + TAIL
    out_shape = (
        [shape((rhs, width), jnp.float32)] * len(rows)
        + [shape((width, depth), jnp.bfloat16)] * sum(new_rows)
        + [
            shape((col.blocks.shape[0], depth, width), jnp.bfloat16)
            for col, is_new in zip(cols, new_cols)
            if is_new
        ]
    )
    made = list(
        pl.pallas_call(
            functools.partial(products_kernel, feat, new_rows, begun, new_cols, groups),
            out_shape=out_shape,
            scratch_shapes=[pltpu.VMEM((width, width), jnp.float32)],
            compiler_params=params(),
            cost_estimate=cost(int(weight * width * width)),
        )(
            lengths,
            *[row.points if row.side is None else row.side for row in rows],
            *[row.partial for row in rows if row.partial is not None],
            *[col.blocks for col in cols],
            *[col.sides for col in cols if col.sides is not None],
        )
    )
    partials = [made.pop(0) for _ in rows]
    sides = [made.pop(0) if is_new else row.side for row, is_new in zip(rows, new_rows)]
    rows = [Row(row.points, side, part) for row, side, part in zip(rows, sides, partials)]
    cols = [Cols(col.blocks, made.pop(0)) if is_new else col for col, is_new in zip(cols, new_cols)]
    return rows, cols


def cost(pairs):
    return pl.CostEstimate(flops=pairs * 768, bytes_accessed=pairs // 4, transcendentals=pairs)


def scattered_kernel(parts, *refs):
    noise_ref, direction_ref, residual_ref = refs[:3]
    image_ref, sums_ref = refs[3 + parts :]
    direction, residual = direction_ref[...], residual_ref[...]
    image = noise_ref[...] * direction
    for ref in refs[3 : 3 + parts]:
        image = image + ref[...]
    image_ref[...] = image
    sums = (
        jnp.sum(residual * residual, axis=1, keepdims=True),
        jnp.sum(direction * image, axis=1, keepdims=True),
        jnp.sum(residual * image, axis=1, keepdims=True),
        jnp.sum(image * image, axis=1, keepdims=True),
    )
    rhs = direction.shape[0]
    lane = lax.broadcasted_iota(jnp.int32, (rhs, 128), 1)
    right = lax.broadcasted_iota(jnp.int32, (rhs, 128), 0)
    packed = jnp.zeros((rhs, 128), jnp.float32)
    for index, value in enumerate(sums):
        packed = jnp.where(lane == index * rhs + right, value, packed)
    row = jnp.sum(packed, axis=0, keepdims=True)
    sums_ref[...] = jnp.broadcast_to(row[None], sums_ref.shape)


def update_kernel(
    solution_ref, residual_ref, direction_ref, image_ref, sums_ref, new_solution, new_residual, new_direction
):
    direction = direction_ref[...]
    rhs = direction.shape[0]
    row = jnp.sum(sums_ref[...], axis=0)
    lane = lax.broadcasted_iota(jnp.int32, (rhs, 128), 1)
    right = lax.broadcasted_iota(jnp.int32, (rhs, 128), 0)
    norm_old, curvature, mixed, image_norm = (
        jnp.sum(jnp.where(lane == index * rhs + right, row, 0.0), axis=1, keepdims=True)
        for index in range(4)
    )
    step = norm_old / curvature
    norm_new = jnp.maximum(norm_old + step * (step * image_norm - 2.0 * mixed), 0.0)
    updated = residual_ref[...] - step * image_ref[...]
    new_solution[...] = solution_ref[...] + step * direction
    new_residual[...] = updated
    new_direction[...] = updated + (norm_new / norm_old) * direction


def swap(array, devices, mask):
    return lax.ppermute(array, AXES, [(at, at ^ mask) for at in range(devices)])


def shift_line(array, devices, steps):
    return lax.ppermute(
        array, AXES, [(at, (at + steps * LINE) % devices) for at in range(devices)]
    )


def local(devices, points, lengths, noise_var, solution, residual, direction):
    f32, bf16 = jnp.float32, jnp.bfloat16
    shape = jax.ShapeDtypeStruct
    feat, width = points.shape
    rhs = direction.shape[0]
    masks = (X + Y, X, Y)
    lengths = lengths[:, None]

    along_x = swap(points, devices, X)
    packed = pl.pallas_call(
        pack_kernel,
        out_shape=shape((feat + rhs, width), bf16),
        in_specs=[pl.BlockSpec(memory_space=pltpu.HBM)] * 2,
        scratch_shapes=[pltpu.VMEM((rhs, width), f32), pltpu.SemaphoreType.DMA((2,))],
        compiler_params=params(),
    )(
        pltpu.with_memory_space_constraint(points, pltpu.HBM),
        pltpu.with_memory_space_constraint(direction, pltpu.HBM),
    )
    pair, near = pl.pallas_call(
        pair_kernel,
        out_shape=[shape((2, feat + rhs, width), bf16), shape((feat, width), bf16)],
        compiler_params=params(),
    )(packed, swap(packed, devices, CORE))
    along_y = swap(near, devices, Y)
    across = swap(along_x, devices, Y)
    add = functools.partial(products, lengths, rhs)

    line = [shift_line(packed, devices, steps) for steps in range(devices // LINE - 1, 0, -1)]
    (own, x_row), (chip,) = add([Row(packed), Row(along_x)], [Cols(pair)], [((0, 1), (0,))], EARLY)
    (x_row, y_row), (_, first) = add(
        [x_row, Row(along_y)], [chip, Cols(line[-1][None])], [((1,), (0,)), ((0, 1), (1,))], EARLY
    )
    (xy_row,), _ = add([Row(across)], [chip, first], [((0,), (0, 1))], EARLY)
    rest = after(xy_row.partial, *line[:-1])
    crossed = swap(after(xy_row.partial, *line), devices, CORE)
    peers, (rest,) = add([xy_row, x_row, y_row], [Cols(rest)], [((0, 1, 2), (0,))], LATE)
    peers, (crossed,) = add(peers, [Cols(crossed)], [((0, 1, 2), (0,))], LATE)
    from_peers = [swap(row.partial, devices, mask) for row, mask in zip(peers, masks)]
    (own,), _ = add([own], [first, rest, crossed], [((0,), (0, 1, 2))], LATE)
    mine = own.partial

    image, sums = pl.pallas_call(
        functools.partial(scattered_kernel, 1 + len(masks)),
        out_shape=[shape((rhs, width), f32), shape((devices, 1, 128), f32)],
        compiler_params=params(),
    )(noise_var[None, :], direction, residual, mine, *from_peers)
    all_sums = lax.all_to_all(sums, AXES, 0, 0, tiled=True)
    return tuple(
        pl.pallas_call(
            update_kernel, out_shape=[shape((rhs, width), f32)] * 3, compiler_params=params()
        )(solution, residual, direction, image, all_sums)
    )


def solution(mesh):
    placed = (
        P(None, AXES),
        P(),
        P(AXES),
        P(None, AXES),
        P(None, AXES),
        P(None, AXES),
    )
    return jax.shard_map(
        functools.partial(local, mesh.shape["row"] * mesh.shape["col"]),
        mesh=mesh,
        in_specs=placed,
        out_specs=(P(None, AXES), P(None, AXES), P(None, AXES)),
        check_vma=False,
    )
```

time: 39.4 us -> 37.8 us (0.959)
  blocking collectives: 10.3 us -> 8.84 us
  Pallas kernels: 10.5 us -> 10.9 us
  starting transfers between devices: 14.7 us -> 14.3 us
    all_to_all x1, blocking collectives: 10.3 us -> 8.84 us  [local(): all_sums = lax.all_to_all(sums, AXES, 0, 0, tiled=True)]
    ppermute x8, starting transfers between devices: 9.21 us -> 8.76 us  [swap(): return lax.ppermute(array, AXES, [(at, at ^ mask) for at in range(devices)])]
    pallas_call x9 -> x11, Pallas kernels: 9.75 us -> 10.1 us  [the longest x6 9 us: products(): pl.pallas_call(functools.partial(products_kernel, feat, new_rows, begun,...]
  transfers between devices with their start and end apart: 11 -> 11, of which waited for: 3 -> 3; matrix products, arithmetic and copies ran while one was open for 0% -> 0% of each run, Pallas kernels for 16% -> 18%
where the time goes in v3:
time: 37.8 us; the launch traced here: 37.6 us
  starting transfers between devices  14.3 us (38%)
  Pallas kernels  10.9 us (29%)
  blocking collectives  8.84 us (23%)
  waiting for transfers between devices  2.76 us (7%)
  between operations  0.73 us (2%)
    pallas_call x6, Pallas kernels, products(): pl.pallas_call(functools.partial(products_kernel, feat, new_rows, begun,...  9 us
    all_to_all x1, blocking collectives, local(): all_sums = lax.all_to_all(sums, AXES, 0, 0, tiled=True)  8.84 us
    ppermute x8, starting transfers between devices, swap(): return lax.ppermute(array, AXES, [(at, at ^ mask) for at in range(devices)])  8.76 us
    ppermute x3, starting transfers between devices, shift_line(): lax.ppermute(array, AXES, [(at, (at + steps * LINE) % devices) for at in...  5.51 us
    ppermute x8, waiting for transfers between devices, swap(): return lax.ppermute(array, AXES, [(at, at ^ mask) for at in range(devices)])  2.75 us
    pallas_call x1, Pallas kernels, local(): pl.pallas_call(pack_kernel, out_shape=shape((feat + rhs, width), bf16), i...  0.93 us
    pallas_call x1, Pallas kernels, local(): pl.pallas_call(update_kernel, out_shape=[shape((rhs, width), f32)] * 3, c...  0.76 us
  transfers between devices with their start and end apart: 11, of which 3 were waited for; matrix products, arithmetic and copies ran while one was open for 0% of the time, Pallas kernels for 18%

profile of v3, /device:TPU:0, one launch (start us, length us, event | category | flops | bytes accessed | tf_op | source)
XLA Modules:
  0.0 37.6 jit_solution(1827925394617471439)
XLA Ops:
  0.6 0.9 %shard_map.85.own_ref.refs_1_ = bf16[80,512]{1,0:T(8,128)(2,1)S(1)} custom-call(bf16[64,512]{1,0:T(8,128)(2,1)} %points_ref.1, f32[16,512]{1,0:T(8,128)} %direction_ref.3), custom_call_target="tpu_custom_call" | custom-call | tf_op jit(solution)/shard_map/pallas_call | solution.py:312
  1.6 0.5 %collective-permute-start.1 = (bf16[80,512]{1,0:T(8,128)(2,1)S(1)}, bf16[80,512]{1,0:T(8,128)(2,1)S(1)}, u32[]{:S(2)}, u32[]{:S(2)}) collective-permute-start(bf16[80,512]{1,0:T(8,128)(2,1)S(1)} %shard_map.85.own_ref.refs_1_), channel_id=1, source_target_pairs={{0,1},{1,0},{2,3},{3,2},{4,5},{5,4},{6,7},{7,6},{8,9},{9,8},{10,11... | collective-permute-start | bytes 245768 | tf_op jit(solution)/shard_map/ppermute | solution.py:294
  2.1 2.6 %collective-permute-start = (bf16[64,512]{1,0:T(8,128)(2,1)S(1)}, bf16[64,512]{1,0:T(8,128)(2,1)S(1)}, u32[]{:S(2)}, u32[]{:S(2)}) collective-permute-start(bf16[64,512]{1,0:T(8,128)(2,1)S(1)} %copy-done.4), channel_id=1, source_target_pairs={{0,2},{1,3},{2,0},{3,1},{4,6},{5,7},{6,4},{7,5},{8,10},{9,11},{10,... | collective-permute-start | bytes 196616 | tf_op jit(solution)/shard_map/ppermute | solution.py:294
  4.7 1.6 %collective-permute-start.2 = (bf16[80,512]{1,0:T(8,128)(2,1)S(1)}, bf16[80,512]{1,0:T(8,128)(2,1)S(1)}, u32[]{:S(2)}, u32[]{:S(2)}) collective-permute-start(bf16[80,512]{1,0:T(8,128)(2,1)S(1)} %shard_map.85.own_ref.refs_1_), channel_id=1, source_target_pairs={{0,8},{1,9},{2,10},{3,11},{4,12},{5,13},{6,14},{7,15},{8,16},{9,17... | collective-permute-start | bytes 245768 | tf_op jit(solution)/shard_map/ppermute | solution.py:298
  6.2 2.6 %collective-permute-start.6 = (bf16[80,512]{1,0:T(8,128)(2,1)S(1)}, bf16[80,512]{1,0:T(8,128)(2,1)S(1)}, u32[]{:S(2)}, u32[]{:S(2)}) collective-permute-start(bf16[80,512]{1,0:T(8,128)(2,1)S(1)} %shard_map.85.own_ref.refs_1_), channel_id=1, source_target_pairs={{0,16},{1,17},{2,18},{3,19},{4,20},{5,21},{6,22},{7,23},{8,24},{9,... | collective-permute-start | bytes 245768 | tf_op jit(solution)/shard_map/ppermute | solution.py:298
  8.8 1.3 %collective-permute-start.5 = (bf16[80,512]{1,0:T(8,128)(2,1)S(1)}, bf16[80,512]{1,0:T(8,128)(2,1)S(1)}, u32[]{:S(2)}, u32[]{:S(2)}) collective-permute-start(bf16[80,512]{1,0:T(8,128)(2,1)S(1)} %shard_map.85.own_ref.refs_1_), channel_id=1, source_target_pairs={{0,24},{1,25},{2,26},{3,27},{4,28},{5,29},{6,30},{7,31},{8,0},{9,1... | collective-permute-start | bytes 245768 | tf_op jit(solution)/shard_map/ppermute | solution.py:298
  10.2 1.6 %collective-permute-start.4 = (bf16[64,512]{1,0:T(8,128)(2,1)S(1)}, bf16[64,512]{1,0:T(8,128)(2,1)S(1)}, u32[]{:S(2)}, u32[]{:S(2)}) collective-permute-start(bf16[64,512]{1,0:T(8,128)(2,1)S(1)} %get-tuple-element.31), channel_id=1, source_target_pairs={{0,4},{1,5},{2,6},{3,7},{4,0},{5,1},{6,2},{7,3},{8,12},{9,13},{10,... | collective-permute-start | bytes 196616 | tf_op jit(solution)/shard_map/ppermute | solution.py:294
  11.8 0.5 %collective-permute-start.3 = (bf16[64,512]{1,0:T(8,128)(2,1)S(1)}, bf16[64,512]{1,0:T(8,128)(2,1)S(1)}, u32[]{:S(2)}, u32[]{:S(2)}) collective-permute-start(bf16[64,512]{1,0:T(8,128)(2,1)S(1)} %collective-permute-done.refs_2_), channel_id=1, source_target_pairs={{0,4},{1,5},{2,6},{3,7},{4,0},{5,1},{6,2},{7,3},{8,12},{9,13},{10,... | collective-permute-start | bytes 196616 | tf_op jit(solution)/shard_map/ppermute | solution.py:294
  12.3 0.1 copy.14.refs_0_
  12.4 1.3 %shard_map.87 = (f32[16,512]{1,0:T(8,128)S(1)}, f32[16,512]{1,0:T(8,128)S(1)}, bf16[512,80]{1,0:T(8,128)(2,1)S(1)}, bf16[512,80]{1,0:T(8,128)(2,1)S(1)}, bf16[2,80,512]{2,1,0:T(8,128)(2,1)S(1)}) custom-call(f32[64,1]{1,0:T(8,128)S(1)} %copy.14.refs_0_, bf16[80,512]{1,0:T(8,128)(2,1)S(1)} %shard_map.85.own_ref.refs_1_, ...), custom_call_target="tpu_custom_call" | custom-call | flops 50331648 | bytes 16384 | tf_op jit(solution)/shard_map/pallas_call | solution.py:224
  13.7 1.2 %collective-permute-done.4.refs_2_ = bf16[64,512]{1,0:T(8,128)(2,1)S(1)} collective-permute-done((bf16[64,512]{1,0:T(8,128)(2,1)S(1)}, bf16[64,512]{1,0:T(8,128)(2,1)S(1)}, u32[]{:S(2)}, u32[]{:S(2)}) %collective-permute-start.4) | collective-permute-done | bytes 65568 | tf_op jit(solution)/shard_map/ppermute | solution.py:294
  14.8 1.2 %shard_map.88 = (f32[16,512]{1,0:T(8,128)S(1)}, f32[16,512]{1,0:T(8,128)S(1)}, bf16[512,80]{1,0:T(8,128)(2,1)S(1)}, bf16[1,80,512]{2,1,0:T(8,128)(2,1)S(1)}) custom-call(f32[64,1]{1,0:T(8,128)S(1)} %copy.14.refs_0_, bf16[512,80]{1,0:T(8,128)(2,1)S(1)} %get-tuple-element.30.refs_1_.refs_2_, bf16[64,512]{1,0:T(8,128)(2,1)S(1)} %collective-permute-done.4.refs_2_, ...), custom_call_target="tpu_custom_call" | custom-call | flops 50331648 | bytes 16384 | tf_op jit(solution)/shard_map/pallas_call | solution.py:224
  16.1 1.0 %shard_map.89 = (f32[16,512]{1,0:T(8,128)S(1)}, bf16[512,80]{1,0:T(8,128)(2,1)S(1)}) custom-call(f32[64,1]{1,0:T(8,128)S(1)} %copy.14.refs_0_, bf16[64,512]{1,0:T(8,128)(2,1)S(1)} %collective-permute-done.3.refs_1_, bf16[2,80,512]{2,1,0:T(8,128)(2,1)S(1)} %get-tuple-element.26.refs_3_.refs_4_.refs_2_, bf16[1,80,512]{2,1,0:T(8,128)(2,1)S(1)} %bitcast.4, ...), custom_call_target="tpu_custom_call" | custom-call | flops 50331648 | bytes 16384 | tf_op jit(solution)/shard_map/pallas_call | solution.py:224
  17.3 1.6 %shard_map.92 = (f32[16,512]{1,0:T(8,128)S(1)}, f32[16,512]{1,0:T(8,128)S(1)}, f32[16,512]{1,0:T(8,128)S(1)}, bf16[2,80,512]{2,1,0:T(8,128)(2,1)S(1)}) custom-call(f32[64,1]{1,0:T(8,128)S(1)} %copy.14.refs_0_, bf16[512,80]{1,0:T(8,128)(2,1)S(1)} %get-tuple-element.35.refs_1_, bf16[512,80]{1,0:T(8,128)(2,1)S(1)} %get-tuple-element.30.refs_1_.refs_2_, ...), custom_call_target="tpu_custom_call" | custom-call | flops 1207959552 | bytes 393216 | tf_op jit(solution)/shard_map/pallas_call | solution.py:224
  18.9 2.3 %shard_map.93 = (f32[16,512]{1,0:T(8,128)S(1)}, f32[16,512]{1,0:T(8,128)S(1)}, f32[16,512]{1,0:T(8,128)S(1)}, bf16[3,80,512]{2,1,0:T(8,128)(2,1)S(1)}) custom-call(f32[64,1]{1,0:T(8,128)S(1)} %copy.14.refs_0_, bf16[512,80]{1,0:T(8,128)(2,1)S(1)} %get-tuple-element.35.refs_1_, bf16[512,80]{1,0:T(8,128)(2,1)S(1)} %get-tuple-element.30.refs_1_.refs_2_, ...), custom_call_target="tpu_custom_call" | custom-call | flops 1207959552 | bytes 393216 | tf_op jit(solution)/shard_map/pallas_call | solution.py:224
  21.2 1.2 %collective-permute-start.8 = (f32[16,512]{1,0:T(8,128)S(1)}, f32[16,512]{1,0:T(8,128)S(1)}, u32[]{:S(2)}, u32[]{:S(2)}) collective-permute-start(f32[16,512]{1,0:T(8,128)S(1)} %get-tuple-element.44), channel_id=1, source_target_pairs={{0,6},{1,7},{2,4},{3,5},{4,2},{5,3},{6,0},{7,1},{8,14},{9,15},{10,... | collective-permute-start | bytes 98312 | tf_op jit(solution)/shard_map/ppermute | solution.py:294
  22.4 1.5 %collective-permute-start.9 = (f32[16,512]{1,0:T(8,128)S(1)}, f32[16,512]{1,0:T(8,128)S(1)}, u32[]{:S(2)}, u32[]{:S(2)}) collective-permute-start(f32[16,512]{1,0:T(8,128)S(1)} %get-tuple-element.45), channel_id=1, source_target_pairs={{0,2},{1,3},{2,0},{3,1},{4,6},{5,7},{6,4},{7,5},{8,10},{9,11},{10,... | collective-permute-start | bytes 98312 | tf_op jit(solution)/shard_map/ppermute | solution.py:294
  23.9 0.8 %collective-permute-start.10 = (f32[16,512]{1,0:T(8,128)S(1)}, f32[16,512]{1,0:T(8,128)S(1)}, u32[]{:S(2)}, u32[]{:S(2)}) collective-permute-start(f32[16,512]{1,0:T(8,128)S(1)} %get-tuple-element.46), channel_id=1, source_target_pairs={{0,4},{1,5},{2,6},{3,7},{4,0},{5,1},{6,2},{7,3},{8,12},{9,13},{10,... | collective-permute-start | bytes 98312 | tf_op jit(solution)/shard_map/ppermute | solution.py:294
  24.7 1.5 %shard_map.94.refs_3_ = f32[16,512]{1,0:T(8,128)S(1)} custom-call(f32[64,1]{1,0:T(8,128)S(1)} %copy.14.refs_0_, bf16[512,80]{1,0:T(8,128)(2,1)S(1)} %get-tuple-element.27.refs_1_, f32[16,512]{1,0:T(8,128)S(1)} %get-tuple-element.28.refs_2_, bf16[1,80,512]{2,1,0:T(8,128)(2,1)S(1)} %bitcast.5, bf16[2,80,512]{2,1,0:T(8,128)(2,1)S(1)} %shard_map.90.refs_7_.refs_4_, ...), custom_call_target="tpu_custom_call" | custom-call | flops 1207959552 | bytes 393216 | tf_op jit(solution)/shard_map/pallas_call | solution.py:224
  26.3 0.1 collective-permute-done.9.refs_5_
  26.4 1.4 %collective-permute-done.10.refs_6_ = f32[16,512]{1,0:T(8,128)S(1)} collective-permute-done((f32[16,512]{1,0:T(8,128)S(1)}, f32[16,512]{1,0:T(8,128)S(1)}, u32[]{:S(2)}, u32[]{:S(2)}) %collective-permute-start.10) | collective-permute-done | bytes 32800 | tf_op jit(solution)/shard_map/ppermute | solution.py:294
  27.8 0.1 shard_map.95
  28.0 8.8 %all_to_all.5.sums_ref = f32[32,1,128]{2,1,0:T(1,128)S(1)} all-to-all(f32[32,1,128]{2,1,0:T(1,128)S(1)} %get-tuple-element.48), channel_id=1, replica_groups=mesh['row'=8,'col'=4] {'row','col'}, dimensions={0} | all-to-all | bytes 32768 | tf_op jit(solution)/shard_map/all_to_all | solution.py:350
  36.8 0.8 %shard_map.96 = (f32[16,512]{1,0:T(8,128)}, f32[16,512]{1,0:T(8,128)}, f32[16,512]{1,0:T(8,128)}) custom-call(f32[16,512]{1,0:T(8,128)S(1)} %copy-done.2, f32[16,512]{1,0:T(8,128)S(1)} %copy-done.1, f32[16,512]{1,0:T(8,128)S(1)} %copy-done, f32[16,512]{1,0:T(8,128)S(1)} %get-tuple-element.47.image_ref, f32[32,1,128]{2,1,0:T(1,128)S(1)} %all_to_all.5.sums_ref), custom_call_target="tpu_custom_call" | custom-call | tf_op jit(solution)/shard_map/pallas_call | solution.py:352
  (24 shorter events, 0.2 us)
Async XLA Ops:
  0.6 1.5 %copy-start.4 = (bf16[64,512]{1,0:T(8,128)(2,1)S(1)}, bf16[64,512]{1,0:T(8,128)(2,1)}, u32[]{:S(2)}) copy-start(bf16[64,512]{1,0:T(8,128)(2,1)} %points_ref.1) | copy-start | bytes 196612
  1.6 8.6 %collective-permute-start.1 = (bf16[80,512]{1,0:T(8,128)(2,1)S(1)}, bf16[80,512]{1,0:T(8,128)(2,1)S(1)}, u32[]{:S(2)}, u32[]{:S(2)}) collective-permute-start(bf16[80,512]{1,0:T(8,128)(2,1)S(1)} %shard_map.85.own_ref.refs_1_), channel_id=1, source_target_pairs={{0,1},{1,0},{2,3},{3,2},{4,5},{5,4},{6,7},{7,6},{8,9},{9,8},{10,11... | collective-permute-start | bytes 245768 | tf_op jit(solution)/shard_map/ppermute | solution.py:294
  2.1 9.7 %collective-permute-start = (bf16[64,512]{1,0:T(8,128)(2,1)S(1)}, bf16[64,512]{1,0:T(8,128)(2,1)S(1)}, u32[]{:S(2)}, u32[]{:S(2)}) collective-permute-start(bf16[64,512]{1,0:T(8,128)(2,1)S(1)} %copy-done.4), channel_id=1, source_target_pairs={{0,2},{1,3},{2,0},{3,1},{4,6},{5,7},{6,4},{7,5},{8,10},{9,11},{10,... | collective-permute-start | bytes 196616 | tf_op jit(solution)/shard_map/ppermute | solution.py:294
  4.7 9.0 %collective-permute-start.2 = (bf16[80,512]{1,0:T(8,128)(2,1)S(1)}, bf16[80,512]{1,0:T(8,128)(2,1)S(1)}, u32[]{:S(2)}, u32[]{:S(2)}) collective-permute-start(bf16[80,512]{1,0:T(8,128)(2,1)S(1)} %shard_map.85.own_ref.refs_1_), channel_id=1, source_target_pairs={{0,8},{1,9},{2,10},{3,11},{4,12},{5,13},{6,14},{7,15},{8,16},{9,17... | collective-permute-start | bytes 245768 | tf_op jit(solution)/shard_map/ppermute | solution.py:298
  6.2 10.9 %collective-permute-start.6 = (bf16[80,512]{1,0:T(8,128)(2,1)S(1)}, bf16[80,512]{1,0:T(8,128)(2,1)S(1)}, u32[]{:S(2)}, u32[]{:S(2)}) collective-permute-start(bf16[80,512]{1,0:T(8,128)(2,1)S(1)} %shard_map.85.own_ref.refs_1_), channel_id=1, source_target_pairs={{0,16},{1,17},{2,18},{3,19},{4,20},{5,21},{6,22},{7,23},{8,24},{9,... | collective-permute-start | bytes 245768 | tf_op jit(solution)/shard_map/ppermute | solution.py:298
  8.8 8.3 %collective-permute-start.5 = (bf16[80,512]{1,0:T(8,128)(2,1)S(1)}, bf16[80,512]{1,0:T(8,128)(2,1)S(1)}, u32[]{:S(2)}, u32[]{:S(2)}) collective-permute-start(bf16[80,512]{1,0:T(8,128)(2,1)S(1)} %shard_map.85.own_ref.refs_1_), channel_id=1, source_target_pairs={{0,24},{1,25},{2,26},{3,27},{4,28},{5,29},{6,30},{7,31},{8,0},{9,1... | collective-permute-start | bytes 245768 | tf_op jit(solution)/shard_map/ppermute | solution.py:298
  10.2 2.1 %copy-start.5 = (f32[64]{0:T(128)S(1)}, f32[64]{0:T(128)}, u32[]{:S(2)}) copy-start(f32[64]{0:T(128)} %param.7) | copy-start | bytes 772
  10.2 4.6 %collective-permute-start.4 = (bf16[64,512]{1,0:T(8,128)(2,1)S(1)}, bf16[64,512]{1,0:T(8,128)(2,1)S(1)}, u32[]{:S(2)}, u32[]{:S(2)}) collective-permute-start(bf16[64,512]{1,0:T(8,128)(2,1)S(1)} %get-tuple-element.31), channel_id=1, source_target_pairs={{0,4},{1,5},{2,6},{3,7},{4,0},{5,1},{6,2},{7,3},{8,12},{9,13},{10,... | collective-permute-start | bytes 196616 | tf_op jit(solution)/shard_map/ppermute | solution.py:294
  11.8 4.3 %collective-permute-start.3 = (bf16[64,512]{1,0:T(8,128)(2,1)S(1)}, bf16[64,512]{1,0:T(8,128)(2,1)S(1)}, u32[]{:S(2)}, u32[]{:S(2)}) collective-permute-start(bf16[64,512]{1,0:T(8,128)(2,1)S(1)} %collective-permute-done.refs_2_), channel_id=1, source_target_pairs={{0,4},{1,5},{2,6},{3,7},{4,0},{5,1},{6,2},{7,3},{8,12},{9,13},{10,... | collective-permute-start | bytes 196616 | tf_op jit(solution)/shard_map/ppermute | solution.py:294
  17.2 1.7 %collective-permute-start.7 = (bf16[3,80,512]{2,1,0:T(8,128)(2,1)S(1)}, bf16[3,80,512]{2,1,0:T(8,128)(2,1)S(1)}, u32[]{:S(2)}, u32[]{:S(2)}) collective-permute-start(bf16[3,80,512]{2,1,0:T(8,128)(2,1)S(1)} %shard_map.91), channel_id=1, source_target_pairs={{0,1},{1,0},{2,3},{3,2},{4,5},{5,4},{6,7},{7,6},{8,9},{9,8},{10,11... | collective-permute-start | bytes 737288 | tf_op jit(solution)/shard_map/ppermute | solution.py:294
  21.2 5.0 %collective-permute-start.8 = (f32[16,512]{1,0:T(8,128)S(1)}, f32[16,512]{1,0:T(8,128)S(1)}, u32[]{:S(2)}, u32[]{:S(2)}) collective-permute-start(f32[16,512]{1,0:T(8,128)S(1)} %get-tuple-element.44), channel_id=1, source_target_pairs={{0,6},{1,7},{2,4},{3,5},{4,2},{5,3},{6,0},{7,1},{8,14},{9,15},{10,... | collective-permute-start | bytes 98312 | tf_op jit(solution)/shard_map/ppermute | solution.py:294
  22.4 4.0 %collective-permute-start.9 = (f32[16,512]{1,0:T(8,128)S(1)}, f32[16,512]{1,0:T(8,128)S(1)}, u32[]{:S(2)}, u32[]{:S(2)}) collective-permute-start(f32[16,512]{1,0:T(8,128)S(1)} %get-tuple-element.45), channel_id=1, source_target_pairs={{0,2},{1,3},{2,0},{3,1},{4,6},{5,7},{6,4},{7,5},{8,10},{9,11},{10,... | collective-permute-start | bytes 98312 | tf_op jit(solution)/shard_map/ppermute | solution.py:294
  23.9 3.9 %collective-permute-start.10 = (f32[16,512]{1,0:T(8,128)S(1)}, f32[16,512]{1,0:T(8,128)S(1)}, u32[]{:S(2)}, u32[]{:S(2)}) collective-permute-start(f32[16,512]{1,0:T(8,128)S(1)} %get-tuple-element.46), channel_id=1, source_target_pairs={{0,4},{1,5},{2,6},{3,7},{4,0},{5,1},{6,2},{7,3},{8,12},{9,13},{10,... | collective-permute-start | bytes 98312 | tf_op jit(solution)/shard_map/ppermute | solution.py:294
  24.7 3.1 %copy-start = (f32[16,512]{1,0:T(8,128)S(1)}, f32[16,512]{1,0:T(8,128)}, u32[]{:S(2)}) copy-start(f32[16,512]{1,0:T(8,128)} %direction_ref.3) | copy-start | bytes 98308
  24.7 3.1 %copy-start.1 = (f32[16,512]{1,0:T(8,128)S(1)}, f32[16,512]{1,0:T(8,128)}, u32[]{:S(2)}) copy-start(f32[16,512]{1,0:T(8,128)} %residual_ref.1) | copy-start | bytes 98308
  24.7 3.1 %copy-start.3 = (f32[512]{0:T(512)S(1)}, f32[512]{0:T(512)}, u32[]{:S(2)}) copy-start(f32[512]{0:T(512)} %param.8) | copy-start | bytes 6148
  28.0 8.9 %copy-start.2 = (f32[16,512]{1,0:T(8,128)S(1)}, f32[16,512]{1,0:T(8,128)}, u32[]{:S(2)}) copy-start(f32[16,512]{1,0:T(8,128)} %solution_ref.1) | copy-start | bytes 98308

commit v4 on v3

--- a/solution.py
+++ b/solution.py
@@ -15,6 +15,7 @@
 LOG2E = 1.4426950408889634
 TAIL = 16
 UNROLL = 16
+AHEAD = 2
 EARLY, LATE = 0.25, 6
 VMEM_LIMIT = 24 * 1024 * 1024
 
@@ -85,13 +86,14 @@
         ]
 
     def run(order, half, last):
+        halves, made = [half], 1
         for place, (out_ref, _, _, weight_ref) in enumerate(order):
-            if place + 1 < len(order):
-                ahead = half_distance(*order[place + 1][1:3])
-            else:
-                ahead = last()
-            add_product(out_ref, half, weight_ref)
-            half = ahead
+            while made < min(place + 1 + AHEAD, len(order)):
+                halves.append(half_distance(*order[made][1:3]))
+                made += 1
+            if place + 1 == len(order):
+                last()
+            add_product(out_ref, halves.pop(0), weight_ref)
 
     pieces = [(rows, sides, blocks) for rows, cols in groups for sides, blocks in cols]
     if sum(len(rows) * sides.shape[0] for rows, sides, _ in pieces) <= UNROLL:

time: 37.8 us -> 38 us (level)
  no operation moved by 1% of the time
where the time goes in v4:
time: 38 us; the launch traced here: 37.8 us
  starting transfers between devices  14.3 us (38%)
  Pallas kernels  11.1 us (29%)
  blocking collectives  8.84 us (23%)
  waiting for transfers between devices  2.7 us (7%)
  between operations  0.73 us (2%)
    pallas_call x6, Pallas kernels, products(): pl.pallas_call(functools.partial(products_kernel, feat, new_rows, begun,...  9.25 us
    all_to_all x1, blocking collectives, local(): all_sums = lax.all_to_all(sums, AXES, 0, 0, tiled=True)  8.84 us
    ppermute x8, starting transfers between devices, swap(): return lax.ppermute(array, AXES, [(at, at ^ mask) for at in range(devices)])  8.76 us
    ppermute x3, starting transfers between devices, shift_line(): lax.ppermute(array, AXES, [(at, (at + steps * LINE) % devices) for at in...  5.51 us
    ppermute x8, waiting for transfers between devices, swap(): return lax.ppermute(array, AXES, [(at, at ^ mask) for at in range(devices)])  2.69 us
    pallas_call x1, Pallas kernels, local(): pl.pallas_call(pack_kernel, out_shape=shape((feat + rhs, width), bf16), i...  0.93 us
    pallas_call x1, Pallas kernels, local(): pl.pallas_call(update_kernel, out_shape=[shape((rhs, width), f32)] * 3, c...  0.76 us
  transfers between devices with their start and end apart: 11, of which 3 were waited for; matrix products, arithmetic and copies ran while one was open for 0% of the time, Pallas kernels for 18%

profile of v4, /device:TPU:0, one launch (start us, length us, event | category | flops | bytes accessed | tf_op | source)
XLA Modules:
  0.0 37.8 jit_solution(16697063449057986498)
XLA Ops:
  0.6 0.9 %shard_map.85.own_ref.refs_1_ = bf16[80,512]{1,0:T(8,128)(2,1)S(1)} custom-call(bf16[64,512]{1,0:T(8,128)(2,1)} %points_ref.1, f32[16,512]{1,0:T(8,128)} %direction_ref.3), custom_call_target="tpu_custom_call" | custom-call | tf_op jit(solution)/shard_map/pallas_call | solution.py:314
  1.6 0.5 %collective-permute-start.1 = (bf16[80,512]{1,0:T(8,128)(2,1)S(1)}, bf16[80,512]{1,0:T(8,128)(2,1)S(1)}, u32[]{:S(2)}, u32[]{:S(2)}) collective-permute-start(bf16[80,512]{1,0:T(8,128)(2,1)S(1)} %shard_map.85.own_ref.refs_1_), channel_id=1, source_target_pairs={{0,1},{1,0},{2,3},{3,2},{4,5},{5,4},{6,7},{7,6},{8,9},{9,8},{10,11... | collective-permute-start | bytes 245768 | tf_op jit(solution)/shard_map/ppermute | solution.py:296
  2.1 2.6 %collective-permute-start = (bf16[64,512]{1,0:T(8,128)(2,1)S(1)}, bf16[64,512]{1,0:T(8,128)(2,1)S(1)}, u32[]{:S(2)}, u32[]{:S(2)}) collective-permute-start(bf16[64,512]{1,0:T(8,128)(2,1)S(1)} %copy-done.4), channel_id=1, source_target_pairs={{0,2},{1,3},{2,0},{3,1},{4,6},{5,7},{6,4},{7,5},{8,10},{9,11},{10,... | collective-permute-start | bytes 196616 | tf_op jit(solution)/shard_map/ppermute | solution.py:296
  4.7 1.6 %collective-permute-start.2 = (bf16[80,512]{1,0:T(8,128)(2,1)S(1)}, bf16[80,512]{1,0:T(8,128)(2,1)S(1)}, u32[]{:S(2)}, u32[]{:S(2)}) collective-permute-start(bf16[80,512]{1,0:T(8,128)(2,1)S(1)} %shard_map.85.own_ref.refs_1_), channel_id=1, source_target_pairs={{0,8},{1,9},{2,10},{3,11},{4,12},{5,13},{6,14},{7,15},{8,16},{9,17... | collective-permute-start | bytes 245768 | tf_op jit(solution)/shard_map/ppermute | solution.py:300
  6.2 2.6 %collective-permute-start.6 = (bf16[80,512]{1,0:T(8,128)(2,1)S(1)}, bf16[80,512]{1,0:T(8,128)(2,1)S(1)}, u32[]{:S(2)}, u32[]{:S(2)}) collective-permute-start(bf16[80,512]{1,0:T(8,128)(2,1)S(1)} %shard_map.85.own_ref.refs_1_), channel_id=1, source_target_pairs={{0,16},{1,17},{2,18},{3,19},{4,20},{5,21},{6,22},{7,23},{8,24},{9,... | collective-permute-start | bytes 245768 | tf_op jit(solution)/shard_map/ppermute | solution.py:300
  8.8 1.3 %collective-permute-start.5 = (bf16[80,512]{1,0:T(8,128)(2,1)S(1)}, bf16[80,512]{1,0:T(8,128)(2,1)S(1)}, u32[]{:S(2)}, u32[]{:S(2)}) collective-permute-start(bf16[80,512]{1,0:T(8,128)(2,1)S(1)} %shard_map.85.own_ref.refs_1_), channel_id=1, source_target_pairs={{0,24},{1,25},{2,26},{3,27},{4,28},{5,29},{6,30},{7,31},{8,0},{9,1... | collective-permute-start | bytes 245768 | tf_op jit(solution)/shard_map/ppermute | solution.py:300
  10.2 1.6 %collective-permute-start.4 = (bf16[64,512]{1,0:T(8,128)(2,1)S(1)}, bf16[64,512]{1,0:T(8,128)(2,1)S(1)}, u32[]{:S(2)}, u32[]{:S(2)}) collective-permute-start(bf16[64,512]{1,0:T(8,128)(2,1)S(1)} %get-tuple-element.31), channel_id=1, source_target_pairs={{0,4},{1,5},{2,6},{3,7},{4,0},{5,1},{6,2},{7,3},{8,12},{9,13},{10,... | collective-permute-start | bytes 196616 | tf_op jit(solution)/shard_map/ppermute | solution.py:296
  11.8 0.5 %collective-permute-start.3 = (bf16[64,512]{1,0:T(8,128)(2,1)S(1)}, bf16[64,512]{1,0:T(8,128)(2,1)S(1)}, u32[]{:S(2)}, u32[]{:S(2)}) collective-permute-start(bf16[64,512]{1,0:T(8,128)(2,1)S(1)} %collective-permute-done.refs_2_), channel_id=1, source_target_pairs={{0,4},{1,5},{2,6},{3,7},{4,0},{5,1},{6,2},{7,3},{8,12},{9,13},{10,... | collective-permute-start | bytes 196616 | tf_op jit(solution)/shard_map/ppermute | solution.py:296
  12.3 0.1 copy.14.refs_0_
  12.4 1.3 %shard_map.87 = (f32[16,512]{1,0:T(8,128)S(1)}, f32[16,512]{1,0:T(8,128)S(1)}, bf16[512,80]{1,0:T(8,128)(2,1)S(1)}, bf16[512,80]{1,0:T(8,128)(2,1)S(1)}, bf16[2,80,512]{2,1,0:T(8,128)(2,1)S(1)}) custom-call(f32[64,1]{1,0:T(8,128)S(1)} %copy.14.refs_0_, bf16[80,512]{1,0:T(8,128)(2,1)S(1)} %shard_map.85.own_ref.refs_1_, ...), custom_call_target="tpu_custom_call" | custom-call | flops 50331648 | bytes 16384 | tf_op jit(solution)/shard_map/pallas_call | solution.py:226
  13.7 1.1 %collective-permute-done.4.refs_2_ = bf16[64,512]{1,0:T(8,128)(2,1)S(1)} collective-permute-done((bf16[64,512]{1,0:T(8,128)(2,1)S(1)}, bf16[64,512]{1,0:T(8,128)(2,1)S(1)}, u32[]{:S(2)}, u32[]{:S(2)}) %collective-permute-start.4) | collective-permute-done | bytes 65568 | tf_op jit(solution)/shard_map/ppermute | solution.py:296
  14.8 1.3 %shard_map.88 = (f32[16,512]{1,0:T(8,128)S(1)}, f32[16,512]{1,0:T(8,128)S(1)}, bf16[512,80]{1,0:T(8,128)(2,1)S(1)}, bf16[1,80,512]{2,1,0:T(8,128)(2,1)S(1)}) custom-call(f32[64,1]{1,0:T(8,128)S(1)} %copy.14.refs_0_, bf16[512,80]{1,0:T(8,128)(2,1)S(1)} %get-tuple-element.30.refs_1_.refs_2_, bf16[64,512]{1,0:T(8,128)(2,1)S(1)} %collective-permute-done.4.refs_2_, ...), custom_call_target="tpu_custom_call" | custom-call | flops 50331648 | bytes 16384 | tf_op jit(solution)/shard_map/pallas_call | solution.py:226
  16.1 1.1 %shard_map.89 = (f32[16,512]{1,0:T(8,128)S(1)}, bf16[512,80]{1,0:T(8,128)(2,1)S(1)}) custom-call(f32[64,1]{1,0:T(8,128)S(1)} %copy.14.refs_0_, bf16[64,512]{1,0:T(8,128)(2,1)S(1)} %collective-permute-done.3.refs_1_, bf16[2,80,512]{2,1,0:T(8,128)(2,1)S(1)} %get-tuple-element.26.refs_3_.refs_4_.refs_2_, bf16[1,80,512]{2,1,0:T(8,128)(2,1)S(1)} %bitcast.4, ...), custom_call_target="tpu_custom_call" | custom-call | flops 50331648 | bytes 16384 | tf_op jit(solution)/shard_map/pallas_call | solution.py:226
  17.3 1.7 %shard_map.92 = (f32[16,512]{1,0:T(8,128)S(1)}, f32[16,512]{1,0:T(8,128)S(1)}, f32[16,512]{1,0:T(8,128)S(1)}, bf16[2,80,512]{2,1,0:T(8,128)(2,1)S(1)}) custom-call(f32[64,1]{1,0:T(8,128)S(1)} %copy.14.refs_0_, bf16[512,80]{1,0:T(8,128)(2,1)S(1)} %get-tuple-element.35.refs_1_, bf16[512,80]{1,0:T(8,128)(2,1)S(1)} %get-tuple-element.30.refs_1_.refs_2_, ...), custom_call_target="tpu_custom_call" | custom-call | flops 1207959552 | bytes 393216 | tf_op jit(solution)/shard_map/pallas_call | solution.py:226
  19.0 2.4 %shard_map.93 = (f32[16,512]{1,0:T(8,128)S(1)}, f32[16,512]{1,0:T(8,128)S(1)}, f32[16,512]{1,0:T(8,128)S(1)}, bf16[3,80,512]{2,1,0:T(8,128)(2,1)S(1)}) custom-call(f32[64,1]{1,0:T(8,128)S(1)} %copy.14.refs_0_, bf16[512,80]{1,0:T(8,128)(2,1)S(1)} %get-tuple-element.35.refs_1_, bf16[512,80]{1,0:T(8,128)(2,1)S(1)} %get-tuple-element.30.refs_1_.refs_2_, ...), custom_call_target="tpu_custom_call" | custom-call | flops 1207959552 | bytes 393216 | tf_op jit(solution)/shard_map/pallas_call | solution.py:226
  21.4 1.2 %collective-permute-start.8 = (f32[16,512]{1,0:T(8,128)S(1)}, f32[16,512]{1,0:T(8,128)S(1)}, u32[]{:S(2)}, u32[]{:S(2)}) collective-permute-start(f32[16,512]{1,0:T(8,128)S(1)} %get-tuple-element.44), channel_id=1, source_target_pairs={{0,6},{1,7},{2,4},{3,5},{4,2},{5,3},{6,0},{7,1},{8,14},{9,15},{10,... | collective-permute-start | bytes 98312 | tf_op jit(solution)/shard_map/ppermute | solution.py:296
  22.6 1.5 %collective-permute-start.9 = (f32[16,512]{1,0:T(8,128)S(1)}, f32[16,512]{1,0:T(8,128)S(1)}, u32[]{:S(2)}, u32[]{:S(2)}) collective-permute-start(f32[16,512]{1,0:T(8,128)S(1)} %get-tuple-element.45), channel_id=1, source_target_pairs={{0,2},{1,3},{2,0},{3,1},{4,6},{5,7},{6,4},{7,5},{8,10},{9,11},{10,... | collective-permute-start | bytes 98312 | tf_op jit(solution)/shard_map/ppermute | solution.py:296
  24.1 0.8 %collective-permute-start.10 = (f32[16,512]{1,0:T(8,128)S(1)}, f32[16,512]{1,0:T(8,128)S(1)}, u32[]{:S(2)}, u32[]{:S(2)}) collective-permute-start(f32[16,512]{1,0:T(8,128)S(1)} %get-tuple-element.46), channel_id=1, source_target_pairs={{0,4},{1,5},{2,6},{3,7},{4,0},{5,1},{6,2},{7,3},{8,12},{9,13},{10,... | collective-permute-start | bytes 98312 | tf_op jit(solution)/shard_map/ppermute | solution.py:296
  24.9 1.5 %shard_map.94.refs_3_ = f32[16,512]{1,0:T(8,128)S(1)} custom-call(f32[64,1]{1,0:T(8,128)S(1)} %copy.14.refs_0_, bf16[512,80]{1,0:T(8,128)(2,1)S(1)} %get-tuple-element.27.refs_1_, f32[16,512]{1,0:T(8,128)S(1)} %get-tuple-element.28.refs_2_, bf16[1,80,512]{2,1,0:T(8,128)(2,1)S(1)} %bitcast.5, bf16[2,80,512]{2,1,0:T(8,128)(2,1)S(1)} %shard_map.90.refs_7_.refs_4_, ...), custom_call_target="tpu_custom_call" | custom-call | flops 1207959552 | bytes 393216 | tf_op jit(solution)/shard_map/pallas_call | solution.py:226
  26.5 0.1 collective-permute-done.9.refs_5_
  26.6 1.5 %collective-permute-done.10.refs_6_ = f32[16,512]{1,0:T(8,128)S(1)} collective-permute-done((f32[16,512]{1,0:T(8,128)S(1)}, f32[16,512]{1,0:T(8,128)S(1)}, u32[]{:S(2)}, u32[]{:S(2)}) %collective-permute-start.10) | collective-permute-done | bytes 32800 | tf_op jit(solution)/shard_map/ppermute | solution.py:296
  28.0 0.1 shard_map.95
  28.2 8.8 %all_to_all.5.sums_ref = f32[32,1,128]{2,1,0:T(1,128)S(1)} all-to-all(f32[32,1,128]{2,1,0:T(1,128)S(1)} %get-tuple-element.48), channel_id=1, replica_groups=mesh['row'=8,'col'=4] {'row','col'}, dimensions={0} | all-to-all | bytes 32768 | tf_op jit(solution)/shard_map/all_to_all | solution.py:352
  37.0 0.8 %shard_map.96 = (f32[16,512]{1,0:T(8,128)}, f32[16,512]{1,0:T(8,128)}, f32[16,512]{1,0:T(8,128)}) custom-call(f32[16,512]{1,0:T(8,128)S(1)} %copy-done.2, f32[16,512]{1,0:T(8,128)S(1)} %copy-done.1, f32[16,512]{1,0:T(8,128)S(1)} %copy-done, f32[16,512]{1,0:T(8,128)S(1)} %get-tuple-element.47.image_ref, f32[32,1,128]{2,1,0:T(1,128)S(1)} %all_to_all.5.sums_ref), custom_call_target="tpu_custom_call" | custom-call | tf_op jit(solution)/shard_map/pallas_call | solution.py:354
  (24 shorter events, 0.2 us)
Async XLA Ops:
  0.6 1.5 %copy-start.4 = (bf16[64,512]{1,0:T(8,128)(2,1)S(1)}, bf16[64,512]{1,0:T(8,128)(2,1)}, u32[]{:S(2)}) copy-start(bf16[64,512]{1,0:T(8,128)(2,1)} %points_ref.1) | copy-start | bytes 196612
  1.6 8.6 %collective-permute-start.1 = (bf16[80,512]{1,0:T(8,128)(2,1)S(1)}, bf16[80,512]{1,0:T(8,128)(2,1)S(1)}, u32[]{:S(2)}, u32[]{:S(2)}) collective-permute-start(bf16[80,512]{1,0:T(8,128)(2,1)S(1)} %shard_map.85.own_ref.refs_1_), channel_id=1, source_target_pairs={{0,1},{1,0},{2,3},{3,2},{4,5},{5,4},{6,7},{7,6},{8,9},{9,8},{10,11... | collective-permute-start | bytes 245768 | tf_op jit(solution)/shard_map/ppermute | solution.py:296
  2.1 9.7 %collective-permute-start = (bf16[64,512]{1,0:T(8,128)(2,1)S(1)}, bf16[64,512]{1,0:T(8,128)(2,1)S(1)}, u32[]{:S(2)}, u32[]{:S(2)}) collective-permute-start(bf16[64,512]{1,0:T(8,128)(2,1)S(1)} %copy-done.4), channel_id=1, source_target_pairs={{0,2},{1,3},{2,0},{3,1},{4,6},{5,7},{6,4},{7,5},{8,10},{9,11},{10,... | collective-permute-start | bytes 196616 | tf_op jit(solution)/shard_map/ppermute | solution.py:296
  4.7 9.1 %collective-permute-start.2 = (bf16[80,512]{1,0:T(8,128)(2,1)S(1)}, bf16[80,512]{1,0:T(8,128)(2,1)S(1)}, u32[]{:S(2)}, u32[]{:S(2)}) collective-permute-start(bf16[80,512]{1,0:T(8,128)(2,1)S(1)} %shard_map.85.own_ref.refs_1_), channel_id=1, source_target_pairs={{0,8},{1,9},{2,10},{3,11},{4,12},{5,13},{6,14},{7,15},{8,16},{9,17... | collective-permute-start | bytes 245768 | tf_op jit(solution)/shard_map/ppermute | solution.py:300
  6.2 11.0 %collective-permute-start.6 = (bf16[80,512]{1,0:T(8,128)(2,1)S(1)}, bf16[80,512]{1,0:T(8,128)(2,1)S(1)}, u32[]{:S(2)}, u32[]{:S(2)}) collective-permute-start(bf16[80,512]{1,0:T(8,128)(2,1)S(1)} %shard_map.85.own_ref.refs_1_), channel_id=1, source_target_pairs={{0,16},{1,17},{2,18},{3,19},{4,20},{5,21},{6,22},{7,23},{8,24},{9,... | collective-permute-start | bytes 245768 | tf_op jit(solution)/shard_map/ppermute | solution.py:300
  8.8 8.4 %collective-permute-start.5 = (bf16[80,512]{1,0:T(8,128)(2,1)S(1)}, bf16[80,512]{1,0:T(8,128)(2,1)S(1)}, u32[]{:S(2)}, u32[]{:S(2)}) collective-permute-start(bf16[80,512]{1,0:T(8,128)(2,1)S(1)} %shard_map.85.own_ref.refs_1_), channel_id=1, source_target_pairs={{0,24},{1,25},{2,26},{3,27},{4,28},{5,29},{6,30},{7,31},{8,0},{9,1... | collective-permute-start | bytes 245768 | tf_op jit(solution)/shard_map/ppermute | solution.py:300
  10.2 2.1 %copy-start.5 = (f32[64]{0:T(128)S(1)}, f32[64]{0:T(128)}, u32[]{:S(2)}) copy-start(f32[64]{0:T(128)} %param.7) | copy-start | bytes 772
  10.2 4.6 %collective-permute-start.4 = (bf16[64,512]{1,0:T(8,128)(2,1)S(1)}, bf16[64,512]{1,0:T(8,128)(2,1)S(1)}, u32[]{:S(2)}, u32[]{:S(2)}) collective-permute-start(bf16[64,512]{1,0:T(8,128)(2,1)S(1)} %get-tuple-element.31), channel_id=1, source_target_pairs={{0,4},{1,5},{2,6},{3,7},{4,0},{5,1},{6,2},{7,3},{8,12},{9,13},{10,... | collective-permute-start | bytes 196616 | tf_op jit(solution)/shard_map/ppermute | solution.py:296
  11.8 4.3 %collective-permute-start.3 = (bf16[64,512]{1,0:T(8,128)(2,1)S(1)}, bf16[64,512]{1,0:T(8,128)(2,1)S(1)}, u32[]{:S(2)}, u32[]{:S(2)}) collective-permute-start(bf16[64,512]{1,0:T(8,128)(2,1)S(1)} %collective-permute-done.refs_2_), channel_id=1, source_target_pairs={{0,4},{1,5},{2,6},{3,7},{4,0},{5,1},{6,2},{7,3},{8,12},{9,13},{10,... | collective-permute-start | bytes 196616 | tf_op jit(solution)/shard_map/ppermute | solution.py:296
  17.2 1.8 %collective-permute-start.7 = (bf16[3,80,512]{2,1,0:T(8,128)(2,1)S(1)}, bf16[3,80,512]{2,1,0:T(8,128)(2,1)S(1)}, u32[]{:S(2)}, u32[]{:S(2)}) collective-permute-start(bf16[3,80,512]{2,1,0:T(8,128)(2,1)S(1)} %shard_map.91), channel_id=1, source_target_pairs={{0,1},{1,0},{2,3},{3,2},{4,5},{5,4},{6,7},{7,6},{8,9},{9,8},{10,11... | collective-permute-start | bytes 737288 | tf_op jit(solution)/shard_map/ppermute | solution.py:296
  21.4 5.1 %collective-permute-start.8 = (f32[16,512]{1,0:T(8,128)S(1)}, f32[16,512]{1,0:T(8,128)S(1)}, u32[]{:S(2)}, u32[]{:S(2)}) collective-permute-start(f32[16,512]{1,0:T(8,128)S(1)} %get-tuple-element.44), channel_id=1, source_target_pairs={{0,6},{1,7},{2,4},{3,5},{4,2},{5,3},{6,0},{7,1},{8,14},{9,15},{10,... | collective-permute-start | bytes 98312 | tf_op jit(solution)/shard_map/ppermute | solution.py:296
  22.6 4.0 %collective-permute-start.9 = (f32[16,512]{1,0:T(8,128)S(1)}, f32[16,512]{1,0:T(8,128)S(1)}, u32[]{:S(2)}, u32[]{:S(2)}) collective-permute-start(f32[16,512]{1,0:T(8,128)S(1)} %get-tuple-element.45), channel_id=1, source_target_pairs={{0,2},{1,3},{2,0},{3,1},{4,6},{5,7},{6,4},{7,5},{8,10},{9,11},{10,... | collective-permute-start | bytes 98312 | tf_op jit(solution)/shard_map/ppermute | solution.py:296
  24.1 3.9 %collective-permute-start.10 = (f32[16,512]{1,0:T(8,128)S(1)}, f32[16,512]{1,0:T(8,128)S(1)}, u32[]{:S(2)}, u32[]{:S(2)}) collective-permute-start(f32[16,512]{1,0:T(8,128)S(1)} %get-tuple-element.46), channel_id=1, source_target_pairs={{0,4},{1,5},{2,6},{3,7},{4,0},{5,1},{6,2},{7,3},{8,12},{9,13},{10,... | collective-permute-start | bytes 98312 | tf_op jit(solution)/shard_map/ppermute | solution.py:296
  24.9 3.1 %copy-start = (f32[16,512]{1,0:T(8,128)S(1)}, f32[16,512]{1,0:T(8,128)}, u32[]{:S(2)}) copy-start(f32[16,512]{1,0:T(8,128)} %direction_ref.3) | copy-start | bytes 98308
  24.9 3.1 %copy-start.1 = (f32[16,512]{1,0:T(8,128)S(1)}, f32[16,512]{1,0:T(8,128)}, u32[]{:S(2)}) copy-start(f32[16,512]{1,0:T(8,128)} %residual_ref.1) | copy-start | bytes 98308
  24.9 3.1 %copy-start.3 = (f32[512]{0:T(512)S(1)}, f32[512]{0:T(512)}, u32[]{:S(2)}) copy-start(f32[512]{0:T(512)} %param.8) | copy-start | bytes 6148
  28.1 8.9 %copy-start.2 = (f32[16,512]{1,0:T(8,128)S(1)}, f32[16,512]{1,0:T(8,128)}, u32[]{:S(2)}) copy-start(f32[16,512]{1,0:T(8,128)} %solution_ref.1) | copy-start | bytes 98308

commit v5 on v3

--- a/solution.py
+++ b/solution.py
@@ -329,7 +329,7 @@
     add = functools.partial(products, lengths, rhs)
 
     line = [shift_line(packed, devices, steps) for steps in range(devices // LINE - 1, 0, -1)]
-    (own, x_row), (chip,) = add([Row(packed), Row(along_x)], [Cols(pair)], [((0, 1), (0,))], EARLY)
+    (x_row,), (chip,) = add([Row(along_x)], [Cols(pair)], [((0,), (0,))], EARLY)
     (x_row, y_row), (_, first) = add(
         [x_row, Row(along_y)], [chip, Cols(line[-1][None])], [((1,), (0,)), ((0, 1), (1,))], EARLY
     )
@@ -339,7 +339,7 @@
     peers, (rest,) = add([xy_row, x_row, y_row], [Cols(rest)], [((0, 1, 2), (0,))], LATE)
     peers, (crossed,) = add(peers, [Cols(crossed)], [((0, 1, 2), (0,))], LATE)
     from_peers = [swap(row.partial, devices, mask) for row, mask in zip(peers, masks)]
-    (own,), _ = add([own], [first, rest, crossed], [((0,), (0, 1, 2))], LATE)
+    (own,), _ = add([Row(packed)], [chip, first, rest, crossed], [((0,), (0, 1, 2, 3))], LATE)
     mine = own.partial
 
     image, sums = pl.pallas_call(

time: 37.8 us -> 38.1 us (level)
  transfers between devices with their start and end apart: 11 -> 11, of which waited for: 3 -> 2; matrix products, arithmetic and copies ran while one was open for 0% -> 0% of each run, Pallas kernels for 18% -> 18%
where the time goes in v5:
time: 38.1 us; the launch traced here: 37.9 us
  starting transfers between devices  14.3 us (38%)
  Pallas kernels  11 us (29%)
  blocking collectives  9.17 us (24%)
  waiting for transfers between devices  2.6 us (7%)
  between operations  0.75 us (2%)
    all_to_all x1, blocking collectives, local(): all_sums = lax.all_to_all(sums, AXES, 0, 0, tiled=True)  9.17 us
    pallas_call x6, Pallas kernels, products(): pl.pallas_call(functools.partial(products_kernel, feat, new_rows, begun,...  9.15 us
    ppermute x8, starting transfers between devices, swap(): return lax.ppermute(array, AXES, [(at, at ^ mask) for at in range(devices)])  8.76 us
    ppermute x3, starting transfers between devices, shift_line(): lax.ppermute(array, AXES, [(at, (at + steps * LINE) % devices) for at in...  5.51 us
    ppermute x8, waiting for transfers between devices, swap(): return lax.ppermute(array, AXES, [(at, at ^ mask) for at in range(devices)])  2.59 us
    pallas_call x1, Pallas kernels, local(): pl.pallas_call(pack_kernel, out_shape=shape((feat + rhs, width), bf16), i...  0.93 us
  transfers between devices with their start and end apart: 11, of which 2 were waited for; matrix products, arithmetic and copies ran while one was open for 0% of the time, Pallas kernels for 18%

profile of v5, /device:TPU:0, one launch (start us, length us, event | category | flops | bytes accessed | tf_op | source)
XLA Modules:
  0.0 37.9 jit_solution(16463204869452457618)
XLA Ops:
  0.6 0.9 %shard_map.85.own_ref.refs_1_ = bf16[80,512]{1,0:T(8,128)(2,1)S(1)} custom-call(bf16[64,512]{1,0:T(8,128)(2,1)} %points_ref.1, f32[16,512]{1,0:T(8,128)} %direction_ref.3), custom_call_target="tpu_custom_call" | custom-call | tf_op jit(solution)/shard_map/pallas_call | solution.py:312
  1.6 0.5 %collective-permute-start = (bf16[80,512]{1,0:T(8,128)(2,1)S(1)}, bf16[80,512]{1,0:T(8,128)(2,1)S(1)}, u32[]{:S(2)}, u32[]{:S(2)}) collective-permute-start(bf16[80,512]{1,0:T(8,128)(2,1)S(1)} %shard_map.85.own_ref.refs_1_), channel_id=1, source_target_pairs={{0,1},{1,0},{2,3},{3,2},{4,5},{5,4},{6,7},{7,6},{8,9},{9,8},{10,11... | collective-permute-start | bytes 245768 | tf_op jit(solution)/shard_map/ppermute | solution.py:294
  2.1 2.6 %collective-permute-start.2 = (bf16[64,512]{1,0:T(8,128)(2,1)S(1)}, bf16[64,512]{1,0:T(8,128)(2,1)S(1)}, u32[]{:S(2)}, u32[]{:S(2)}) collective-permute-start(bf16[64,512]{1,0:T(8,128)(2,1)S(1)} %copy-done.4), channel_id=1, source_target_pairs={{0,2},{1,3},{2,0},{3,1},{4,6},{5,7},{6,4},{7,5},{8,10},{9,11},{10,... | collective-permute-start | bytes 196616 | tf_op jit(solution)/shard_map/ppermute | solution.py:294
  4.7 1.6 %collective-permute-start.1 = (bf16[80,512]{1,0:T(8,128)(2,1)S(1)}, bf16[80,512]{1,0:T(8,128)(2,1)S(1)}, u32[]{:S(2)}, u32[]{:S(2)}) collective-permute-start(bf16[80,512]{1,0:T(8,128)(2,1)S(1)} %shard_map.85.own_ref.refs_1_), channel_id=1, source_target_pairs={{0,8},{1,9},{2,10},{3,11},{4,12},{5,13},{6,14},{7,15},{8,16},{9,17... | collective-permute-start | bytes 245768 | tf_op jit(solution)/shard_map/ppermute | solution.py:298
  6.2 2.6 %collective-permute-start.6 = (bf16[80,512]{1,0:T(8,128)(2,1)S(1)}, bf16[80,512]{1,0:T(8,128)(2,1)S(1)}, u32[]{:S(2)}, u32[]{:S(2)}) collective-permute-start(bf16[80,512]{1,0:T(8,128)(2,1)S(1)} %shard_map.85.own_ref.refs_1_), channel_id=1, source_target_pairs={{0,16},{1,17},{2,18},{3,19},{4,20},{5,21},{6,22},{7,23},{8,24},{9,... | collective-permute-start | bytes 245768 | tf_op jit(solution)/shard_map/ppermute | solution.py:298
  8.8 1.3 %collective-permute-start.5 = (bf16[80,512]{1,0:T(8,128)(2,1)S(1)}, bf16[80,512]{1,0:T(8,128)(2,1)S(1)}, u32[]{:S(2)}, u32[]{:S(2)}) collective-permute-start(bf16[80,512]{1,0:T(8,128)(2,1)S(1)} %shard_map.85.own_ref.refs_1_), channel_id=1, source_target_pairs={{0,24},{1,25},{2,26},{3,27},{4,28},{5,29},{6,30},{7,31},{8,0},{9,1... | collective-permute-start | bytes 245768 | tf_op jit(solution)/shard_map/ppermute | solution.py:298
  10.2 1.6 %collective-permute-start.4 = (bf16[64,512]{1,0:T(8,128)(2,1)S(1)}, bf16[64,512]{1,0:T(8,128)(2,1)S(1)}, u32[]{:S(2)}, u32[]{:S(2)}) collective-permute-start(bf16[64,512]{1,0:T(8,128)(2,1)S(1)} %get-tuple-element.28), channel_id=1, source_target_pairs={{0,4},{1,5},{2,6},{3,7},{4,0},{5,1},{6,2},{7,3},{8,12},{9,13},{10,... | collective-permute-start | bytes 196616 | tf_op jit(solution)/shard_map/ppermute | solution.py:294
  11.8 0.5 %collective-permute-start.3 = (bf16[64,512]{1,0:T(8,128)(2,1)S(1)}, bf16[64,512]{1,0:T(8,128)(2,1)S(1)}, u32[]{:S(2)}, u32[]{:S(2)}) collective-permute-start(bf16[64,512]{1,0:T(8,128)(2,1)S(1)} %collective-permute-done.2.refs_1_), channel_id=1, source_target_pairs={{0,4},{1,5},{2,6},{3,7},{4,0},{5,1},{6,2},{7,3},{8,12},{9,13},{10,... | collective-permute-start | bytes 196616 | tf_op jit(solution)/shard_map/ppermute | solution.py:294
  12.3 0.1 copy.14.refs_0_
  12.4 0.8 %shard_map.87 = (f32[16,512]{1,0:T(8,128)S(1)}, bf16[512,80]{1,0:T(8,128)(2,1)S(1)}, bf16[2,80,512]{2,1,0:T(8,128)(2,1)S(1)}) custom-call(f32[64,1]{1,0:T(8,128)S(1)} %copy.14.refs_0_, bf16[64,512]{1,0:T(8,128)(2,1)S(1)} %collective-permute-done.2.refs_1_, bf16[2,80,512]{2,1,0:T(8,128)(2,1)S(1)} %get-tuple-element.25.refs_2_.refs_4_), custom_call_target="tpu_custom_call" | custom-call | flops 50331648 | bytes 16384 | tf_op jit(solution)/shard_map/pallas_call | solution.py:224
  13.2 1.6 %collective-permute-done.4.refs_2_ = bf16[64,512]{1,0:T(8,128)(2,1)S(1)} collective-permute-done((bf16[64,512]{1,0:T(8,128)(2,1)S(1)}, bf16[64,512]{1,0:T(8,128)(2,1)S(1)}, u32[]{:S(2)}, u32[]{:S(2)}) %collective-permute-start.4) | collective-permute-done | bytes 65568 | tf_op jit(solution)/shard_map/ppermute | solution.py:294
  14.8 1.2 %shard_map.88 = (f32[16,512]{1,0:T(8,128)S(1)}, f32[16,512]{1,0:T(8,128)S(1)}, bf16[512,80]{1,0:T(8,128)(2,1)S(1)}, bf16[1,80,512]{2,1,0:T(8,128)(2,1)S(1)}) custom-call(f32[64,1]{1,0:T(8,128)S(1)} %copy.14.refs_0_, bf16[512,80]{1,0:T(8,128)(2,1)S(1)} %get-tuple-element.27.refs_1_.refs_2_, bf16[64,512]{1,0:T(8,128)(2,1)S(1)} %collective-permute-done.4.refs_2_, ...), custom_call_target="tpu_custom_call" | custom-call | flops 50331648 | bytes 16384 | tf_op jit(solution)/shard_map/pallas_call | solution.py:224
  16.1 1.0 %shard_map.89 = (f32[16,512]{1,0:T(8,128)S(1)}, bf16[512,80]{1,0:T(8,128)(2,1)S(1)}) custom-call(f32[64,1]{1,0:T(8,128)S(1)} %copy.14.refs_0_, bf16[64,512]{1,0:T(8,128)(2,1)S(1)} %collective-permute-done.3.refs_1_, bf16[2,80,512]{2,1,0:T(8,128)(2,1)S(1)} %get-tuple-element.25.refs_2_.refs_4_, bf16[1,80,512]{2,1,0:T(8,128)(2,1)S(1)} %bitcast.4, ...), custom_call_target="tpu_custom_call" | custom-call | flops 50331648 | bytes 16384 | tf_op jit(solution)/shard_map/pallas_call | solution.py:224
  17.2 0.1 collective-permute-start.7
  17.3 1.6 %shard_map.92 = (f32[16,512]{1,0:T(8,128)S(1)}, f32[16,512]{1,0:T(8,128)S(1)}, f32[16,512]{1,0:T(8,128)S(1)}, bf16[2,80,512]{2,1,0:T(8,128)(2,1)S(1)}) custom-call(f32[64,1]{1,0:T(8,128)S(1)} %copy.14.refs_0_, bf16[512,80]{1,0:T(8,128)(2,1)S(1)} %get-tuple-element.32.refs_1_, bf16[512,80]{1,0:T(8,128)(2,1)S(1)} %get-tuple-element.27.refs_1_.refs_2_, ...), custom_call_target="tpu_custom_call" | custom-call | flops 1207959552 | bytes 393216 | tf_op jit(solution)/shard_map/pallas_call | solution.py:224
  18.9 2.3 %shard_map.93 = (f32[16,512]{1,0:T(8,128)S(1)}, f32[16,512]{1,0:T(8,128)S(1)}, f32[16,512]{1,0:T(8,128)S(1)}, bf16[3,80,512]{2,1,0:T(8,128)(2,1)S(1)}) custom-call(f32[64,1]{1,0:T(8,128)S(1)} %copy.14.refs_0_, bf16[512,80]{1,0:T(8,128)(2,1)S(1)} %get-tuple-element.32.refs_1_, bf16[512,80]{1,0:T(8,128)(2,1)S(1)} %get-tuple-element.27.refs_1_.refs_2_, ...), custom_call_target="tpu_custom_call" | custom-call | flops 1207959552 | bytes 393216 | tf_op jit(solution)/shard_map/pallas_call | solution.py:224
  21.2 1.2 %collective-permute-start.8 = (f32[16,512]{1,0:T(8,128)S(1)}, f32[16,512]{1,0:T(8,128)S(1)}, u32[]{:S(2)}, u32[]{:S(2)}) collective-permute-start(f32[16,512]{1,0:T(8,128)S(1)} %get-tuple-element.42), channel_id=1, source_target_pairs={{0,6},{1,7},{2,4},{3,5},{4,2},{5,3},{6,0},{7,1},{8,14},{9,15},{10,... | collective-permute-start | bytes 98312 | tf_op jit(solution)/shard_map/ppermute | solution.py:294
  22.4 1.5 %collective-permute-start.9 = (f32[16,512]{1,0:T(8,128)S(1)}, f32[16,512]{1,0:T(8,128)S(1)}, u32[]{:S(2)}, u32[]{:S(2)}) collective-permute-start(f32[16,512]{1,0:T(8,128)S(1)} %get-tuple-element.43), channel_id=1, source_target_pairs={{0,2},{1,3},{2,0},{3,1},{4,6},{5,7},{6,4},{7,5},{8,10},{9,11},{10,... | collective-permute-start | bytes 98312 | tf_op jit(solution)/shard_map/ppermute | solution.py:294
  23.9 0.8 %collective-permute-start.10 = (f32[16,512]{1,0:T(8,128)S(1)}, f32[16,512]{1,0:T(8,128)S(1)}, u32[]{:S(2)}, u32[]{:S(2)}) collective-permute-start(f32[16,512]{1,0:T(8,128)S(1)} %get-tuple-element.44), channel_id=1, source_target_pairs={{0,4},{1,5},{2,6},{3,7},{4,0},{5,1},{6,2},{7,3},{8,12},{9,13},{10,... | collective-permute-start | bytes 98312 | tf_op jit(solution)/shard_map/ppermute | solution.py:294
  24.7 2.1 %shard_map.94 = (f32[16,512]{1,0:T(8,128)S(1)}, bf16[512,80]{1,0:T(8,128)(2,1)}) custom-call(f32[64,1]{1,0:T(8,128)S(1)} %copy.14.refs_0_, bf16[80,512]{1,0:T(8,128)(2,1)S(1)} %shard_map.85.own_ref.refs_1_, bf16[2,80,512]{2,1,0:T(8,128)(2,1)S(1)} %get-tuple-element.25.refs_2_.refs_4_, bf16[1,80,512]{2,1,0:T(8,128)(2,1)S(1)} %bitcast.5, ...), custom_call_target="tpu_custom_call" | custom-call | flops 1207959552 | bytes 393216 | tf_op jit(solution)/shard_map/pallas_call | solution.py:224
  26.9 0.9 %collective-permute-done.10.refs_6_ = f32[16,512]{1,0:T(8,128)S(1)} collective-permute-done((f32[16,512]{1,0:T(8,128)S(1)}, f32[16,512]{1,0:T(8,128)S(1)}, u32[]{:S(2)}, u32[]{:S(2)}) %collective-permute-start.10) | collective-permute-done | bytes 32800 | tf_op jit(solution)/shard_map/ppermute | solution.py:294
  27.8 0.1 shard_map.95
  28.0 9.2 %all_to_all.5.sums_ref = f32[32,1,128]{2,1,0:T(1,128)S(1)} all-to-all(f32[32,1,128]{2,1,0:T(1,128)S(1)} %get-tuple-element.46), channel_id=1, replica_groups=mesh['row'=8,'col'=4] {'row','col'}, dimensions={0} | all-to-all | bytes 32768 | tf_op jit(solution)/shard_map/all_to_all | solution.py:350
  37.1 0.8 %shard_map.96 = (f32[16,512]{1,0:T(8,128)}, f32[16,512]{1,0:T(8,128)}, f32[16,512]{1,0:T(8,128)}) custom-call(f32[16,512]{1,0:T(8,128)S(1)} %copy-done.2, f32[16,512]{1,0:T(8,128)S(1)} %copy-done.1, f32[16,512]{1,0:T(8,128)S(1)} %copy-done, f32[16,512]{1,0:T(8,128)S(1)} %get-tuple-element.45.image_ref, f32[32,1,128]{2,1,0:T(1,128)S(1)} %all_to_all.5.sums_ref), custom_call_target="tpu_custom_call" | custom-call | tf_op jit(solution)/shard_map/pallas_call | solution.py:352
  (24 shorter events, 0.1 us)
Async XLA Ops:
  0.6 1.5 %copy-start.4 = (bf16[64,512]{1,0:T(8,128)(2,1)S(1)}, bf16[64,512]{1,0:T(8,128)(2,1)}, u32[]{:S(2)}) copy-start(bf16[64,512]{1,0:T(8,128)(2,1)} %points_ref.1) | copy-start | bytes 196612
  1.6 8.6 %collective-permute-start = (bf16[80,512]{1,0:T(8,128)(2,1)S(1)}, bf16[80,512]{1,0:T(8,128)(2,1)S(1)}, u32[]{:S(2)}, u32[]{:S(2)}) collective-permute-start(bf16[80,512]{1,0:T(8,128)(2,1)S(1)} %shard_map.85.own_ref.refs_1_), channel_id=1, source_target_pairs={{0,1},{1,0},{2,3},{3,2},{4,5},{5,4},{6,7},{7,6},{8,9},{9,8},{10,11... | collective-permute-start | bytes 245768 | tf_op jit(solution)/shard_map/ppermute | solution.py:294
  2.1 9.7 %collective-permute-start.2 = (bf16[64,512]{1,0:T(8,128)(2,1)S(1)}, bf16[64,512]{1,0:T(8,128)(2,1)S(1)}, u32[]{:S(2)}, u32[]{:S(2)}) collective-permute-start(bf16[64,512]{1,0:T(8,128)(2,1)S(1)} %copy-done.4), channel_id=1, source_target_pairs={{0,2},{1,3},{2,0},{3,1},{4,6},{5,7},{6,4},{7,5},{8,10},{9,11},{10,... | collective-permute-start | bytes 196616 | tf_op jit(solution)/shard_map/ppermute | solution.py:294
  4.7 8.5 %collective-permute-start.1 = (bf16[80,512]{1,0:T(8,128)(2,1)S(1)}, bf16[80,512]{1,0:T(8,128)(2,1)S(1)}, u32[]{:S(2)}, u32[]{:S(2)}) collective-permute-start(bf16[80,512]{1,0:T(8,128)(2,1)S(1)} %shard_map.85.own_ref.refs_1_), channel_id=1, source_target_pairs={{0,8},{1,9},{2,10},{3,11},{4,12},{5,13},{6,14},{7,15},{8,16},{9,17... | collective-permute-start | bytes 245768 | tf_op jit(solution)/shard_map/ppermute | solution.py:298
  6.2 10.9 %collective-permute-start.6 = (bf16[80,512]{1,0:T(8,128)(2,1)S(1)}, bf16[80,512]{1,0:T(8,128)(2,1)S(1)}, u32[]{:S(2)}, u32[]{:S(2)}) collective-permute-start(bf16[80,512]{1,0:T(8,128)(2,1)S(1)} %shard_map.85.own_ref.refs_1_), channel_id=1, source_target_pairs={{0,16},{1,17},{2,18},{3,19},{4,20},{5,21},{6,22},{7,23},{8,24},{9,... | collective-permute-start | bytes 245768 | tf_op jit(solution)/shard_map/ppermute | solution.py:298
  8.8 8.3 %collective-permute-start.5 = (bf16[80,512]{1,0:T(8,128)(2,1)S(1)}, bf16[80,512]{1,0:T(8,128)(2,1)S(1)}, u32[]{:S(2)}, u32[]{:S(2)}) collective-permute-start(bf16[80,512]{1,0:T(8,128)(2,1)S(1)} %shard_map.85.own_ref.refs_1_), channel_id=1, source_target_pairs={{0,24},{1,25},{2,26},{3,27},{4,28},{5,29},{6,30},{7,31},{8,0},{9,1... | collective-permute-start | bytes 245768 | tf_op jit(solution)/shard_map/ppermute | solution.py:298
  10.2 2.1 %copy-start.5 = (f32[64]{0:T(128)S(1)}, f32[64]{0:T(128)}, u32[]{:S(2)}) copy-start(f32[64]{0:T(128)} %param.7) | copy-start | bytes 772
  10.2 4.6 %collective-permute-start.4 = (bf16[64,512]{1,0:T(8,128)(2,1)S(1)}, bf16[64,512]{1,0:T(8,128)(2,1)S(1)}, u32[]{:S(2)}, u32[]{:S(2)}) collective-permute-start(bf16[64,512]{1,0:T(8,128)(2,1)S(1)} %get-tuple-element.28), channel_id=1, source_target_pairs={{0,4},{1,5},{2,6},{3,7},{4,0},{5,1},{6,2},{7,3},{8,12},{9,13},{10,... | collective-permute-start | bytes 196616 | tf_op jit(solution)/shard_map/ppermute | solution.py:294
  11.8 4.3 %collective-permute-start.3 = (bf16[64,512]{1,0:T(8,128)(2,1)S(1)}, bf16[64,512]{1,0:T(8,128)(2,1)S(1)}, u32[]{:S(2)}, u32[]{:S(2)}) collective-permute-start(bf16[64,512]{1,0:T(8,128)(2,1)S(1)} %collective-permute-done.2.refs_1_), channel_id=1, source_target_pairs={{0,4},{1,5},{2,6},{3,7},{4,0},{5,1},{6,2},{7,3},{8,12},{9,13},{10,... | collective-permute-start | bytes 196616 | tf_op jit(solution)/shard_map/ppermute | solution.py:294
  17.2 1.7 %collective-permute-start.7 = (bf16[3,80,512]{2,1,0:T(8,128)(2,1)S(1)}, bf16[3,80,512]{2,1,0:T(8,128)(2,1)S(1)}, u32[]{:S(2)}, u32[]{:S(2)}) collective-permute-start(bf16[3,80,512]{2,1,0:T(8,128)(2,1)S(1)} %shard_map.91), channel_id=1, source_target_pairs={{0,1},{1,0},{2,3},{3,2},{4,5},{5,4},{6,7},{7,6},{8,9},{9,8},{10,11... | collective-permute-start | bytes 737288 | tf_op jit(solution)/shard_map/ppermute | solution.py:294
  21.2 5.7 %collective-permute-start.8 = (f32[16,512]{1,0:T(8,128)S(1)}, f32[16,512]{1,0:T(8,128)S(1)}, u32[]{:S(2)}, u32[]{:S(2)}) collective-permute-start(f32[16,512]{1,0:T(8,128)S(1)} %get-tuple-element.42), channel_id=1, source_target_pairs={{0,6},{1,7},{2,4},{3,5},{4,2},{5,3},{6,0},{7,1},{8,14},{9,15},{10,... | collective-permute-start | bytes 98312 | tf_op jit(solution)/shard_map/ppermute | solution.py:294
  22.4 4.5 %collective-permute-start.9 = (f32[16,512]{1,0:T(8,128)S(1)}, f32[16,512]{1,0:T(8,128)S(1)}, u32[]{:S(2)}, u32[]{:S(2)}) collective-permute-start(f32[16,512]{1,0:T(8,128)S(1)} %get-tuple-element.43), channel_id=1, source_target_pairs={{0,2},{1,3},{2,0},{3,1},{4,6},{5,7},{6,4},{7,5},{8,10},{9,11},{10,... | collective-permute-start | bytes 98312 | tf_op jit(solution)/shard_map/ppermute | solution.py:294
  23.9 3.9 %collective-permute-start.10 = (f32[16,512]{1,0:T(8,128)S(1)}, f32[16,512]{1,0:T(8,128)S(1)}, u32[]{:S(2)}, u32[]{:S(2)}) collective-permute-start(f32[16,512]{1,0:T(8,128)S(1)} %get-tuple-element.44), channel_id=1, source_target_pairs={{0,4},{1,5},{2,6},{3,7},{4,0},{5,1},{6,2},{7,3},{8,12},{9,13},{10,... | collective-permute-start | bytes 98312 | tf_op jit(solution)/shard_map/ppermute | solution.py:294
  24.7 3.1 %copy-start = (f32[16,512]{1,0:T(8,128)S(1)}, f32[16,512]{1,0:T(8,128)}, u32[]{:S(2)}) copy-start(f32[16,512]{1,0:T(8,128)} %direction_ref.3) | copy-start | bytes 98308
  24.7 3.1 %copy-start.1 = (f32[16,512]{1,0:T(8,128)S(1)}, f32[16,512]{1,0:T(8,128)}, u32[]{:S(2)}) copy-start(f32[16,512]{1,0:T(8,128)} %residual_ref.1) | copy-start | bytes 98308
  26.9 1.0 %copy-start.3 = (f32[512]{0:T(512)S(1)}, f32[512]{0:T(512)}, u32[]{:S(2)}) copy-start(f32[512]{0:T(512)} %param.8) | copy-start | bytes 6148
  28.0 9.2 %copy-start.2 = (f32[16,512]{1,0:T(8,128)S(1)}, f32[16,512]{1,0:T(8,128)}, u32[]{:S(2)}) copy-start(f32[16,512]{1,0:T(8,128)} %solution_ref.1) | copy-start | bytes 98308
